TPU v7x, 128 devices: a whole 4x4x4 slice. The times are simulated.
128 devices in a mesh: row: 16 (over y, z), col: 8 (over x, core).
Axes of the slice: x: 4, y: 4, z: 4, core: 2. Of those that a mesh axis runs over, the one named last changes fastest.
Arguments:
- amplitude: float32 [512, 256, 256], P(('row', 'col')), may hold values from 0.1 to 3
- patches: float32 [512, 2, 256, 256], P(('row', 'col')), may hold values from -5 to 5
- dual: float32 [512, 3, 2, 256, 256], P(('row', 'col')), may hold values from -3 to 3
- probe: float32 [3, 2, 256, 256], replicated, may hold values from -6 to 6
- obj: float32 [2, 12288, 6144], P(None, 'row', 'col'), may hold values from -5 to 5
- positions: int32 [512, 2], P(('row', 'col')), may hold values from 0 to 12032, as said below
Outputs:
- dual_new: float32 [512, 3, 2, 256, 256], P(('row', 'col'))
- object_new: float32 [2, 12288, 6144], P(None, 'row', 'col')
- probe_new: float32 [3, 2, 256, 256], replicated
- patches_new: float32 [512, 2, 256, 256], P(('row', 'col'))
Inputs may be any that keep to these rules, and one draw needn't show every extreme that they name: `positions`: both entries of each row are multiples of 128. A frame held by the device at index i of row and j of col has its row offset between i * 768 and (i + 1) * 768 - 128 and its column offset between j * 768 and (j + 1) * 768 - 128; every frame lies inside the object.
All inputs are finite; a program needn't handle non-finite values.
Results may differ from a plain program's by a relative error of at most 0.0003.
Values sent between devices are 32-bit elements; how exact they have to be, the bound alone decides.
A program may use at most 192 MiB of HBM per device.

v0:
```python
import math
import numpy as np
import ml_dtypes
import jax
import jax.numpy as jnp
from jax import lax
from jax.experimental import pallas as pl
from jax.experimental.pallas import tpu as pltpu
from jax.sharding import PartitionSpec as P

N = 256
H = 128
MODES = 3
TILE = 768
WIDE = TILE + H
F32, BF16 = jnp.float32, jnp.bfloat16


def dft_tables():
    k = np.arange(H)
    stacked = []
    for odd in (0, 1):
        angle = ((2 * k[:, None] + odd) * k[None, :] % N) * (2.0 * math.pi / N)
        c, s = np.cos(angle) / 16.0, np.sin(angle) / 16.0
        stacked.append(np.block([[c, s], [-s, c]]))
    whole = np.stack(stacked + [t.T for t in stacked]).astype(np.float32)
    lead = whole.astype(ml_dtypes.bfloat16)
    rest = (whole - lead.astype(np.float32)).astype(ml_dtypes.bfloat16)
    return np.stack([lead, rest], axis=1)


def order_table():
    t = np.zeros((N, N), np.float32)
    k = np.arange(H)
    t[2 * k, k] = 1.0
    t[2 * k + 1, H + k] = 1.0
    return np.stack([t, t.T]).astype(ml_dtypes.bfloat16)


def parts(x):
    lead = x.astype(BF16)
    return lead, (x - lead.astype(F32)).astype(BF16)


def dot(a, b):
    return lax.dot_general(a, b, (((1,), (0,)), ((), ())), preferred_element_type=F32)


def left(tab, which, x):
    lead, rest = parts(x)
    a, b = tab[which, 0], tab[which, 1]
    return dot(jnp.concatenate([a, a, b], axis=1), jnp.concatenate([lead, rest, lead], axis=0))


def right(tab, which, x):
    lead, rest = parts(x)
    a, b = tab[which, 0], tab[which, 1]
    return dot(jnp.concatenate([lead, rest, lead], axis=1), jnp.concatenate([a, a, b], axis=0))


def top(x):
    return x[:H]


def bot(x):
    return x[H:]


def lft(x):
    return x[:, :H]


def rgt(x):
    return x[:, H:]


def rows2(a, b):
    return jnp.concatenate([a, b], axis=0)


def cols2(a, b):
    return jnp.concatenate([a, b], axis=1)


def forward(tab, xr, xi):
    e = left(tab, 0, rows2(top(xr) + bot(xr), top(xi) + bot(xi)))
    o = left(tab, 1, rows2(top(xr) - bot(xr), top(xi) - bot(xi)))
    yr, yi = rows2(top(e), top(o)), rows2(bot(e), bot(o))
    even = right(tab, 2, cols2(lft(yr) + rgt(yr), lft(yi) + rgt(yi)))
    odd = right(tab, 3, cols2(lft(yr) - rgt(yr), lft(yi) - rgt(yi)))
    return even, odd


def inverse(tab, even, odd):
    a = right(tab, 0, even)
    b = right(tab, 1, odd)
    yr = cols2(lft(a) + lft(b), lft(a) - lft(b))
    yi = cols2(rgt(a) + rgt(b), rgt(a) - rgt(b))
    e = left(tab, 2, rows2(top(yr), top(yi)))
    o = left(tab, 3, rows2(bot(yr), bot(yi)))
    xr = rows2(top(e) + top(o), top(e) - top(o))
    xi = rows2(bot(e) + bot(o), bot(e) - bot(o))
    return xr, xi


def frame_kernel(place, amp, patches, dual, probe, tab, order, dual_new, canvas, sums, far):
    f = pl.program_id(0)

    @pl.when(f == 0)
    def _():
        canvas[...] = jnp.zeros_like(canvas)
        sums[...] = jnp.zeros_like(sums)

    pr, pi = patches[0, 0], patches[0, 1]
    sums[6] += pr * pr + pi * pi
    power_e = power_o = None
    for m in range(MODES):
        qr, qi = probe[m, 0], probe[m, 1]
        xr = qr * pr - qi * pi + dual[0, m, 0]
        xi = qr * pi + qi * pr + dual[0, m, 1]
        even, odd = forward(tab, xr, xi)
        far[m, 0] = even
        far[m, 1] = odd
        e2 = lft(even) * lft(even) + rgt(even) * rgt(even)
        o2 = lft(odd) * lft(odd) + rgt(odd) * rgt(odd)
        power_e = e2 if power_e is None else power_e + e2
        power_o = o2 if power_o is None else power_o + o2
    lead, rest = parts(amp[0])
    a = dot(cols2(order[1], order[1]), rows2(lead, rest))
    lead, rest = parts(a)
    a = dot(cols2(lead, rest), rows2(order[0], order[0]))
    ratio_e = lft(a) * lax.rsqrt(power_e + 1.0)
    ratio_o = rgt(a) * lax.rsqrt(power_o + 1.0)
    ratio_e, ratio_o = cols2(ratio_e, ratio_e), cols2(ratio_o, ratio_o)
    obj_re = obj_im = None
    for m in range(MODES):
        qr, qi = probe[m, 0], probe[m, 1]
        nr, ni = inverse(tab, far[m, 0] * ratio_e, far[m, 1] * ratio_o)
        dr = dual[0, m, 0] + (qr * pr - qi * pi) - nr
        di = dual[0, m, 1] + (qr * pi + qi * pr) - ni
        dual_new[0, m, 0] = dr
        dual_new[0, m, 1] = di
        tr, ti = nr - dr, ni - di
        sums[2 * m] += pr * tr + pi * ti
        sums[2 * m + 1] += pr * ti - pi * tr
        re = qr * tr + qi * ti
        im = qr * ti - qi * tr
        obj_re = re if obj_re is None else obj_re + re
        obj_im = im if obj_im is None else obj_im + im
    r = pl.multiple_of(place[f, 0], H)
    c = pl.multiple_of(place[f, 1], H)
    canvas[0, pl.ds(r, N), pl.ds(c, N)] += obj_re
    canvas[1, pl.ds(r, N), pl.ds(c, N)] += obj_im
    square = probe[...] * probe[...]
    canvas[2, pl.ds(r, N), pl.ds(c, N)] += jnp.sum(square, axis=(0, 1))


def frames(place, amp, patches, dual, probe):
    n = amp.shape[0]
    tab, order = jnp.asarray(dft_tables()), jnp.asarray(order_table())
    whole = lambda *d: pl.BlockSpec(d, lambda f, p: (0,) * len(d))
    grid = pltpu.PrefetchScalarGridSpec(
        num_scalar_prefetch=1,
        grid=(n,),
        in_specs=[
            pl.BlockSpec((1, N, N), lambda f, p: (f, 0, 0)),
            pl.BlockSpec((1, 2, N, N), lambda f, p: (f, 0, 0, 0)),
            pl.BlockSpec((1, MODES, 2, N, N), lambda f, p: (f, 0, 0, 0, 0)),
            whole(MODES, 2, N, N),
            whole(4, 2, N, N),
            whole(2, N, N),
        ],
        out_specs=[
            pl.BlockSpec((1, MODES, 2, N, N), lambda f, p: (f, 0, 0, 0, 0)),
            whole(3, WIDE, WIDE),
            whole(7, N, N),
        ],
        scratch_shapes=[pltpu.VMEM((MODES, 2, N, N), F32)],
    )
    return pl.pallas_call(
        frame_kernel,
        grid_spec=grid,
        out_shape=[
            jax.ShapeDtypeStruct(dual.shape, F32),
            jax.ShapeDtypeStruct((3, WIDE, WIDE), F32),
            jax.ShapeDtypeStruct((7, N, N), F32),
        ],
        compiler_params=pltpu.CompilerParams(vmem_limit_bytes=56 << 20),
    )(place, amp, patches, dual, probe, tab, order)


SWEEPS = 4


amp_floor = 1.0
obj_weight = 0.5
smooth_weight = 16.0
probe_weight = 1.0


def from_behind(block, axis, distance):
    devices = range(lax.axis_size(axis))
    route = [(i - distance, i) for i in devices if i - distance in devices]
    return lax.ppermute(block, axis, route)


def extended_2(block, sides, width):
    for axis, dim in sides:
        count = lax.axis_size(axis)
        forward = [(i, i + 1) for i in range(count - 1)]
        backward = [(target, source) for source, target in forward]
        low = lax.ppermute(
            lax.slice_in_dim(block, block.shape[dim] - width, None, axis=dim), axis, forward
        )
        high = lax.ppermute(lax.slice_in_dim(block, 0, width, axis=dim), axis, backward)
        block = jnp.concatenate([low, block, high], axis=dim)
    return block


def neighbours(padded):
    return padded[:, 2:, 1:-1] + padded[:, :-2, 1:-1] + padded[:, 1:-1, 2:] + padded[:, 1:-1, :-2]


def per_device(amplitude, patches, dual, probe, obj, positions):
    width = amplitude.shape[-1]
    half_width = width // 2
    modes = probe.shape[0]
    tile = obj.shape[1]
    row_index = lax.axis_index("row")
    col_index = lax.axis_index("col")
    origin = jnp.stack([row_index, col_index]).astype(jnp.int32) * tile
    place = positions - origin
    dual_new, canvas, sums = frames(place, amplitude, patches, dual, probe)
    packed = sums.reshape(7, width * width)
    probe_flat = probe.reshape(2 * modes, width * width)
    totals = lax.psum(packed, ("row", "col"))
    probe_new = (
        (totals[: 2 * modes] + probe_weight * probe_flat) / (totals[2 * modes :] + probe_weight)
    ).reshape(probe.shape)
    local_rows = place[:, 0]
    local_cols = place[:, 1]
    anchor = jnp.zeros((), jnp.int32)

    from_left = from_behind(canvas[:, :, tile:], "col", 1)
    canvas = canvas.at[:, :, :half_width].add(from_left)
    from_above = from_behind(canvas[:, tile:, :tile], "row", 1)
    sums_own = canvas[:, :tile, :tile].at[:, :half_width, :].add(from_above)
    rhs = sums_own[:2] + obj_weight * obj
    diagonal = sums_own[2] + obj_weight + 4.0 * smooth_weight
    field = obj
    for sweep in range(SWEEPS):
        padded = extended_2(field, (("row", 1), ("col", 2)), 1)
        field = (rhs + smooth_weight * neighbours(padded)) / diagonal
    from_right = from_behind(field[:, :, :half_width], "col", -1)
    wider = jnp.concatenate([field, from_right], axis=2)
    from_below = from_behind(wider[:, :half_width, :], "row", -1)
    extended = jnp.concatenate([wider, from_below], axis=1)

    def window(row_start, col_start):
        return lax.dynamic_slice(extended, (anchor, row_start, col_start), (2, width, width))

    patches_new = jax.vmap(window)(local_rows, local_cols)
    return (dual_new, field, probe_new, patches_new)


def solution(mesh):
    return jax.shard_map(
        per_device,
        mesh=mesh,
        in_specs=(
            P(("row", "col"), None, None),
            P(("row", "col"), None, None, None),
            P(("row", "col"), None, None, None, None),
            P(),
            P(None, "row", "col"),
            P(("row", "col"), None),
        ),
        out_specs=(
            P(("row", "col"), None, None, None, None),
            P(None, "row", "col"),
            P(),
            P(("row", "col"), None, None, None),
        ),
        check_vma=False,
    )
```

profile of v0, /device:TPU:0, one launch (start us, length us, event | category | flops | bytes accessed | tf_op | source)
XLA Modules:
  0.0 381.5 jit_solution(16388101798954321767)
XLA Ops:
  8.7 28.9 %shard_map.111 = (f32[4,3,2,256,256]{4,3,2,1,0:T(8,128)}, f32[3,896,896]{2,1,0:T(8,128)}, f32[7,256,256]{2,1,0:T(8,128)}) custom-call(s32[4,2]{1,0:T(4,128)} %broadcast_subtract_fusion.place, f32[4,256,256]{2,1,0:T(8,128)} %amp.1, f32[4,2,256,256]{3,2,1,0:T(8,128)} %patches.1, f32[4,3,2,256,256]{4,3,2,1,0:T(8,128)} %dual.1, f32[3,2,256,256]{3,2,1,0:T(8,128)} %probe.1, ...), custom_call_target="tpu_custom_call" | custom-call | tf_op jit(solution)/shard_map/pallas_call | solution.py:180
  40.4 2.6 collective-permute-done
  43.0 2.7 add_dynamic-update-slice_fusion
  45.7 2.4 slice.256
  48.0 4.4 %collective-permute-start.1 = (f32[3,128,768]{2,1,0:T(8,128)}, f32[3,128,768]{2,1,0:T(8,128)S(1)}, u32[]{:S(2)}, u32[]{:S(2)}) collective-permute-start(f32[3,128,768]{2,1,0:T(8,128)} %slice.256), channel_id=1, source_target_pairs={{0,8},{8,16},{16,24},{24,32},{32,40},{40,48},{48,56},{56,64},{64,7... | collective-permute-start | bytes 3538952 | tf_op jit(solution)/shard_map/ppermute | solution.py:204
  53.8 4.5 %collective-permute-start.3 = (f32[2,1,768]{2,1,0:T(1,128)S(1)}, f32[2,1,768]{2,1,0:T(1,128)S(1)}, u32[]{:S(2)}, u32[]{:S(2)}) collective-permute-start(f32[2,1,768]{2,1,0:T(1,128)S(1)} %get-tuple-element.66), channel_id=1, source_target_pairs={{0,8},{8,16},{16,24},{24,32},{32,40},{40,48},{48,56},{56,64},{64,7... | collective-permute-start | bytes 18440 | tf_op jit(solution)/shard_map/ppermute | solution.py:212
  58.3 8.0 %collective-permute-done.3 = f32[2,1,768]{2,1,0:T(1,128)S(1)} collective-permute-done((f32[2,1,768]{2,1,0:T(1,128)S(1)}, f32[2,1,768]{2,1,0:T(1,128)S(1)}, u32[]{:S(2)}, u32[]{:S(2)}) %collective-permute-start.3) | collective-permute-done | bytes 6176 | tf_op jit(solution)/shard_map/ppermute | solution.py:212
  68.6 15.9 %collective-permute-start.5 = (f32[2,770,1]{1,0,2:T(2,128)S(1)}, f32[2,770,1]{1,0,2:T(2,128)S(1)}, u32[]{:S(2)}, u32[]{:S(2)}) collective-permute-start(f32[2,770,1]{1,0,2:T(2,128)S(1)} %copy.16), channel_id=1, source_target_pairs={{0,1},{1,2},{2,3},{3,4},{4,5},{5,6},{6,7},{8,9},{9,10},{10,11},{11... | collective-permute-start | bytes 18488 | tf_op jit(solution)/shard_map/ppermute | solution.py:212
  86.9 3.7 slice.254
  92.4 7.2 %fusion.21 = f32[2,768,768]{2,1,0:T(8,128)S(1)} fusion(f32[2,770,1]{2,1,0:T(8,128)S(1)} %copy-done.5, f32[2,1,768]{2,1,0:T(1,128)S(1)} %collective-permute-done.2, f32[2,768,768]{2,1,0:T(8,128)S(1)} %bitcast.26, f32[2,1,768]{2,1,0:T(1,128)S(1)} %collective-permute-done.3, f32[2,770,1]{2,1,0:T(8,128)S(1)} %copy-done.4, f32[768,768]{1,0:T(8,128)S(1)} %fusion.24, ...), kind=kLoop, calls=%fused_computation.49 | loop fusion | flops 18874368 | bytes 16539680 | tf_op jit(solution)/shard_map/div | solution.py:253
  100.9 4.7 %collective-permute-start.7 = (f32[2,1,768]{2,1,0:T(1,128)S(1)}, f32[2,1,768]{2,1,0:T(1,128)S(1)}, u32[]{:S(2)}, u32[]{:S(2)}) collective-permute-start(f32[2,1,768]{2,1,0:T(1,128)S(1)} %get-tuple-element.64), channel_id=1, source_target_pairs={{0,8},{8,16},{16,24},{24,32},{32,40},{40,48},{48,56},{56,64},{64,7... | collective-permute-start | bytes 18440 | tf_op jit(solution)/shard_map/ppermute | solution.py:212
  112.5 16.4 %collective-permute-start.9 = (f32[2,770,1]{1,0,2:T(2,128)S(1)}, f32[2,770,1]{1,0,2:T(2,128)S(1)}, u32[]{:S(2)}, u32[]{:S(2)}) collective-permute-start(f32[2,770,1]{1,0,2:T(2,128)S(1)} %copy.20), channel_id=1, source_target_pairs={{0,1},{1,2},{2,3},{3,4},{4,5},{5,6},{6,7},{8,9},{9,10},{10,11},{11... | collective-permute-start | bytes 18488 | tf_op jit(solution)/shard_map/ppermute | solution.py:212
  131.4 13.3 %fusion.15 = f32[2,768,768]{2,1,0:T(8,128)S(1)} fusion(f32[2,770,1]{2,1,0:T(8,128)} %copy.21, f32[2,1,768]{2,1,0:T(1,128)S(1)} %collective-permute-done.6, f32[2,768,768]{2,1,0:T(8,128)} %copy-done.2, f32[2,1,768]{2,1,0:T(1,128)S(1)} %collective-permute-done.7, f32[2,770,1]{2,1,0:T(8,128)} %copy.19, f32[768,768]{1,0:T(8,128)S(1)} %fusion.24, ...), kind=kLoop, calls=%fused_computation.35 | loop fusion | flops 18874368 | bytes 21258272 | tf_op jit(solution)/shard_map/div | solution.py:253
  146.1 4.5 %collective-permute-start.11 = (f32[2,1,768]{2,1,0:T(1,128)S(1)}, f32[2,1,768]{2,1,0:T(1,128)S(1)}, u32[]{:S(2)}, u32[]{:S(2)}) collective-permute-start(f32[2,1,768]{2,1,0:T(1,128)S(1)} %get-tuple-element.62), channel_id=1, source_target_pairs={{0,8},{8,16},{16,24},{24,32},{32,40},{40,48},{48,56},{56,64},{64,7... | collective-permute-start | bytes 18440 | tf_op jit(solution)/shard_map/ppermute | solution.py:212
  157.6 4.6 %collective-permute-start.13 = (f32[2,770,1]{1,0,2:T(2,128)S(1)}, f32[2,770,1]{1,0,2:T(2,128)S(1)}, u32[]{:S(2)}, u32[]{:S(2)}) collective-permute-start(f32[2,770,1]{1,0,2:T(2,128)S(1)} %copy.24), channel_id=1, source_target_pairs={{0,1},{1,2},{2,3},{3,4},{4,5},{5,6},{6,7},{8,9},{9,10},{10,11},{11... | collective-permute-start | bytes 18488 | tf_op jit(solution)/shard_map/ppermute | solution.py:212
  162.2 3.9 %copy.30 = f32[1,7,256,256]{3,1,2,0:T(8,128)} copy(f32[1,7,256,256]{3,2,1,0:T(8,128)} %bitcast.31) | data formatting | bytes 3670016
  168.5 14.9 %fusion.9 = f32[2,768,768]{2,1,0:T(8,128)} fusion(f32[2,770,1]{2,1,0:T(8,128)} %copy.25, f32[2,1,768]{2,1,0:T(1,128)S(1)} %collective-permute-done.10, f32[2,768,768]{2,1,0:T(8,128)} %copy-done.1, f32[2,1,768]{2,1,0:T(1,128)S(1)} %collective-permute-done.11, f32[2,770,1]{2,1,0:T(8,128)} %copy.23, f32[768,768]{1,0:T(8,128)S(1)} %fusion.24, ...), kind=kLoop, calls=%fused_computation.21 | loop fusion | flops 18874368 | bytes 21258272 | tf_op jit(solution)/shard_map/div | solution.py:253
  185.5 4.5 %collective-permute-start.15 = (f32[2,1,768]{2,1,0:T(1,128)S(1)}, f32[2,1,768]{2,1,0:T(1,128)S(1)}, u32[]{:S(2)}, u32[]{:S(2)}) collective-permute-start(f32[2,1,768]{2,1,0:T(1,128)S(1)} %get-tuple-element.60), channel_id=1, source_target_pairs={{0,8},{8,16},{16,24},{24,32},{32,40},{40,48},{48,56},{56,64},{64,7... | collective-permute-start | bytes 18440 | tf_op jit(solution)/shard_map/ppermute | solution.py:212
  191.4 2.8 pad_maximum_fusion.36
  198.4 4.6 %collective-permute-start.17 = (f32[2,770,1]{1,0,2:T(2,128)S(1)}, f32[2,770,1]{1,0,2:T(2,128)S(1)}, u32[]{:S(2)}, u32[]{:S(2)}) collective-permute-start(f32[2,770,1]{1,0,2:T(2,128)S(1)} %copy.28), channel_id=1, source_target_pairs={{0,1},{1,2},{2,3},{3,4},{4,5},{5,6},{6,7},{8,9},{9,10},{10,11},{11... | collective-permute-start | bytes 18488 | tf_op jit(solution)/shard_map/ppermute | solution.py:212
  203.1 3.7 copy.31
  209.3 14.7 %fusion.3 = f32[2,768,768]{2,1,0:T(8,128)} fusion(f32[2,770,1]{2,1,0:T(8,128)} %copy.29, f32[2,1,768]{2,1,0:T(1,128)S(1)} %collective-permute-done.14, f32[2,768,768]{2,1,0:T(8,128)} %fusion.9, f32[2,1,768]{2,1,0:T(1,128)S(1)} %collective-permute-done.15, f32[2,770,1]{2,1,0:T(8,128)} %copy.27, f32[768,768]{1,0:T(8,128)S(1)} %fusion.24, ...), kind=kLoop, calls=%fused_computation.7 | loop fusion | flops 18874368 | bytes 21258272 | tf_op jit(solution)/shard_map/div | solution.py:253
  224.0 2.2 slice.267
  227.5 98.0 %all-reduce.2.cloned.1.call-done = f32[7,65536]{1,0:T(8,128)} async-done(((f32[7,65536]{1,0:T(8,128)}), f32[7,65536]{1,0:T(8,128)}) %all-reduce.2.cloned.1.call-update) | async-done | bytes 1835024 | tf_op jit(solution)/shard_map/psum | solution.py:236
  325.5 2.1 slice_add_fusion.4
  332.1 20.6 %collective-permute-done.19 = f32[2,128,896]{2,1,0:T(8,128)S(1)} collective-permute-done((f32[2,128,896]{2,1,0:T(8,128)S(1)}, f32[2,128,896]{2,1,0:T(8,128)S(1)}, u32[]{:S(2)}, u32[]{:S(2)}) %collective-permute-start.19) | collective-permute-done | bytes 917536 | tf_op jit(solution)/shard_map/ppermute | solution.py:204
  352.8 5.5 %pad_maximum_fusion = f32[2,896,896]{2,1,0:T(8,128)} fusion(f32[2,128,896]{2,1,0:T(8,128)S(1)} %collective-permute-done.19, f32[2,768,128]{2,1,0:T(8,128)S(1)} %collective-permute-done.18, f32[2,768,768]{2,1,0:T(8,128)} %fusion.3), kind=kLoop, calls=%fused_computation.2 | loop fusion | flops 3211264 | bytes 12845056 | tf_op jit(solution)/shard_map/concatenate | solution.py:257
  358.2 16.4 %while.3 = (s32[]{:T(128)}, f32[2,896,896]{2,1,0:T(8,128)}, s32[4,3]{1,0:T(4,128)S(1)}, f32[4,2,256,256]{3,2,1,0:T(8,128)}, s32[]{:T(128)}) while((s32[]{:T(128)}, f32[2,896,896]{2,1,0:T(8,128)}, s32[4,3]{1,0:T(4,128)S(1)}, f32[4,2,256,256]{3,2,1,0:T(8,128)}, s32[]{:T(128)}) %tuple.40), condition=%wide.while_cond.2, body=%wide.while_body.2.sunk | while | flops 2 | bytes 1050217 | solution.py:260
  358.9 3.4 bitcast_dynamic-update-slice_fusion.2
  363.0 3.4 bitcast_dynamic-update-slice_fusion.2
  367.1 3.4 bitcast_dynamic-update-slice_fusion.2
  371.2 3.4 bitcast_dynamic-update-slice_fusion.2
  (100 shorter events, 51.8 us)
Async XLA Ops:
  7.2 318.4 %all-reduce.2.cloned.1.call-start = ((), (), s32[]{:S(2)}) async-start(), calls=%async_computation | async-start | bytes 4194304 | tf_op jit(solution)/shard_map/psum | solution.py:236
  8.1 44.4 %slice-start = ((s8[4718592]{0:T(1024)(128)(4,1)}), s8[4194304]{0:T(1024)(128)(4,1)S(1)}, s32[]{:S(2)}) async-start(s8[4718592]{0:T(1024)(128)(4,1)} %bitcast.23), calls=%async_computation.1 | async-start | bytes 8388608
  8.7 43.8 %slice-start.1 = ((s8[4718592]{0:T(1024)(128)(4,1)}), s8[524288]{0:T(1024)(128)(4,1)S(1)}, s32[]{:S(2)}) async-start(s8[4718592]{0:T(1024)(128)(4,1)} %bitcast.23), calls=%async_computation.2 | async-start | bytes 1048576
  39.0 4.0 %collective-permute-start = (f32[3,896,128]{2,1,0:T(8,128)S(1)}, f32[3,896,128]{2,1,0:T(8,128)S(1)}, u32[]{:S(2)}, u32[]{:S(2)}) collective-permute-start(f32[3,896,128]{2,1,0:T(8,128)S(1)} %slice.195), channel_id=1, source_target_pairs={{0,1},{1,2},{2,3},{3,4},{4,5},{5,6},{6,7},{8,9},{9,10},{10,11},{11... | collective-permute-start | bytes 4128776 | tf_op jit(solution)/shard_map/ppermute | solution.py:204
  48.0 42.5 %collective-permute-start.1 = (f32[3,128,768]{2,1,0:T(8,128)}, f32[3,128,768]{2,1,0:T(8,128)S(1)}, u32[]{:S(2)}, u32[]{:S(2)}) collective-permute-start(f32[3,128,768]{2,1,0:T(8,128)} %slice.256), channel_id=1, source_target_pairs={{0,8},{8,16},{16,24},{24,32},{32,40},{40,48},{48,56},{56,64},{64,7... | collective-permute-start | bytes 3538952 | tf_op jit(solution)/shard_map/ppermute | solution.py:204
  52.5 5.9 %collective-permute-start.2 = (f32[2,1,768]{2,1,0:T(1,128)S(1)}, f32[2,1,768]{2,1,0:T(1,128)S(1)}, u32[]{:S(2)}, u32[]{:S(2)}) collective-permute-start(f32[2,1,768]{2,1,0:T(1,128)S(1)} %get-tuple-element.67), channel_id=1, source_target_pairs={{8,0},{16,8},{24,16},{32,24},{40,32},{48,40},{56,48},{64,56},{72,6... | collective-permute-start | bytes 18440 | tf_op jit(solution)/shard_map/ppermute | solution.py:215
  53.8 12.6 %collective-permute-start.3 = (f32[2,1,768]{2,1,0:T(1,128)S(1)}, f32[2,1,768]{2,1,0:T(1,128)S(1)}, u32[]{:S(2)}, u32[]{:S(2)}) collective-permute-start(f32[2,1,768]{2,1,0:T(1,128)S(1)} %get-tuple-element.66), channel_id=1, source_target_pairs={{0,8},{8,16},{16,24},{24,32},{32,40},{40,48},{48,56},{56,64},{64,7... | collective-permute-start | bytes 18440 | tf_op jit(solution)/shard_map/ppermute | solution.py:212
  67.0 17.5 %collective-permute-start.4 = (f32[2,770,1]{1,0,2:T(2,128)S(1)}, f32[2,770,1]{1,0,2:T(2,128)S(1)}, u32[]{:S(2)}, u32[]{:S(2)}) collective-permute-start(f32[2,770,1]{1,0,2:T(2,128)S(1)} %copy.14), channel_id=1, source_target_pairs={{1,0},{2,1},{3,2},{4,3},{5,4},{6,5},{7,6},{9,8},{10,9},{11,10},{12... | collective-permute-start | bytes 18488 | tf_op jit(solution)/shard_map/ppermute | solution.py:215
  68.6 17.1 %collective-permute-start.5 = (f32[2,770,1]{1,0,2:T(2,128)S(1)}, f32[2,770,1]{1,0,2:T(2,128)S(1)}, u32[]{:S(2)}, u32[]{:S(2)}) collective-permute-start(f32[2,770,1]{1,0,2:T(2,128)S(1)} %copy.16), channel_id=1, source_target_pairs={{0,1},{1,2},{2,3},{3,4},{4,5},{5,6},{6,7},{8,9},{9,10},{10,11},{11... | collective-permute-start | bytes 18488 | tf_op jit(solution)/shard_map/ppermute | solution.py:212
  85.7 6.6 %slice-start.2 = ((s8[4718592]{0:T(1024)(128)(4,1)}), s8[524288]{0:T(1024)(128)(4,1)S(1)}, s32[]{:S(2)}) async-start(s8[4718592]{0:T(1024)(128)(4,1)} %bitcast.25), calls=%async_computation.3 | async-start | bytes 1048576
  86.9 5.4 %slice-start.3 = ((s8[4718592]{0:T(1024)(128)(4,1)}), s8[4194304]{0:T(1024)(128)(4,1)S(1)}, s32[]{:S(2)}) async-start(s8[4718592]{0:T(1024)(128)(4,1)} %bitcast.25), calls=%async_computation.4 | async-start | bytes 8388608
  90.5 1.9 copy-start.5
  92.1 7.5 %copy-start = (f32[3,768,768]{2,1,0:T(8,128)}, f32[3,768,768]{2,1,0:T(8,128)S(1)}, u32[]{:S(2)}) copy-start(f32[3,768,768]{2,1,0:T(8,128)S(1)} %fusion.26) | copy-start | bytes 21233668
  99.6 7.4 %copy-start.2 = (f32[2,768,768]{2,1,0:T(8,128)}, f32[2,768,768]{2,1,0:T(8,128)S(1)}, u32[]{:S(2)}) copy-start(f32[2,768,768]{2,1,0:T(8,128)S(1)} %fusion.21) | copy-start | bytes 14155780
  99.6 6.0 %collective-permute-start.6 = (f32[2,1,768]{2,1,0:T(1,128)S(1)}, f32[2,1,768]{2,1,0:T(1,128)S(1)}, u32[]{:S(2)}, u32[]{:S(2)}) collective-permute-start(f32[2,1,768]{2,1,0:T(1,128)S(1)} %get-tuple-element.65), channel_id=1, source_target_pairs={{8,0},{16,8},{24,16},{32,24},{40,32},{48,40},{56,48},{64,56},{72,6... | collective-permute-start | bytes 18440 | tf_op jit(solution)/shard_map/ppermute | solution.py:215
  100.9 6.0 %collective-permute-start.7 = (f32[2,1,768]{2,1,0:T(1,128)S(1)}, f32[2,1,768]{2,1,0:T(1,128)S(1)}, u32[]{:S(2)}, u32[]{:S(2)}) collective-permute-start(f32[2,1,768]{2,1,0:T(1,128)S(1)} %get-tuple-element.64), channel_id=1, source_target_pairs={{0,8},{8,16},{16,24},{24,32},{32,40},{40,48},{48,56},{56,64},{64,7... | collective-permute-start | bytes 18440 | tf_op jit(solution)/shard_map/ppermute | solution.py:212
  109.8 19.1 %collective-permute-start.8 = (f32[2,770,1]{1,0,2:T(2,128)S(1)}, f32[2,770,1]{1,0,2:T(2,128)S(1)}, u32[]{:S(2)}, u32[]{:S(2)}) collective-permute-start(f32[2,770,1]{1,0,2:T(2,128)S(1)} %copy.18), channel_id=1, source_target_pairs={{1,0},{2,1},{3,2},{4,3},{5,4},{6,5},{7,6},{9,8},{10,9},{11,10},{12... | collective-permute-start | bytes 18488 | tf_op jit(solution)/shard_map/ppermute | solution.py:215
  112.5 17.7 %collective-permute-start.9 = (f32[2,770,1]{1,0,2:T(2,128)S(1)}, f32[2,770,1]{1,0,2:T(2,128)S(1)}, u32[]{:S(2)}, u32[]{:S(2)}) collective-permute-start(f32[2,770,1]{1,0,2:T(2,128)S(1)} %copy.20), channel_id=1, source_target_pairs={{0,1},{1,2},{2,3},{3,4},{4,5},{5,6},{6,7},{8,9},{9,10},{10,11},{11... | collective-permute-start | bytes 18488 | tf_op jit(solution)/shard_map/ppermute | solution.py:212
  144.7 7.2 %copy-start.1 = (f32[2,768,768]{2,1,0:T(8,128)}, f32[2,768,768]{2,1,0:T(8,128)S(1)}, u32[]{:S(2)}) copy-start(f32[2,768,768]{2,1,0:T(8,128)S(1)} %fusion.15) | copy-start | bytes 14155780
  144.8 5.9 %collective-permute-start.10 = (f32[2,1,768]{2,1,0:T(1,128)S(1)}, f32[2,1,768]{2,1,0:T(1,128)S(1)}, u32[]{:S(2)}, u32[]{:S(2)}) collective-permute-start(f32[2,1,768]{2,1,0:T(1,128)S(1)} %get-tuple-element.63), channel_id=1, source_target_pairs={{8,0},{16,8},{24,16},{32,24},{40,32},{48,40},{56,48},{64,56},{72,6... | collective-permute-start | bytes 18440 | tf_op jit(solution)/shard_map/ppermute | solution.py:215
  146.1 5.9 %collective-permute-start.11 = (f32[2,1,768]{2,1,0:T(1,128)S(1)}, f32[2,1,768]{2,1,0:T(1,128)S(1)}, u32[]{:S(2)}, u32[]{:S(2)}) collective-permute-start(f32[2,1,768]{2,1,0:T(1,128)S(1)} %get-tuple-element.62), channel_id=1, source_target_pairs={{0,8},{8,16},{16,24},{24,32},{32,40},{40,48},{48,56},{56,64},{64,7... | collective-permute-start | bytes 18440 | tf_op jit(solution)/shard_map/ppermute | solution.py:212
  154.8 11.3 %collective-permute-start.12 = (f32[2,770,1]{1,0,2:T(2,128)S(1)}, f32[2,770,1]{1,0,2:T(2,128)S(1)}, u32[]{:S(2)}, u32[]{:S(2)}) collective-permute-start(f32[2,770,1]{1,0,2:T(2,128)S(1)} %copy.22), channel_id=1, source_target_pairs={{1,0},{2,1},{3,2},{4,3},{5,4},{6,5},{7,6},{9,8},{10,9},{11,10},{12... | collective-permute-start | bytes 18488 | tf_op jit(solution)/shard_map/ppermute | solution.py:215
  157.6 9.8 %collective-permute-start.13 = (f32[2,770,1]{1,0,2:T(2,128)S(1)}, f32[2,770,1]{1,0,2:T(2,128)S(1)}, u32[]{:S(2)}, u32[]{:S(2)}) collective-permute-start(f32[2,770,1]{1,0,2:T(2,128)S(1)} %copy.24), channel_id=1, source_target_pairs={{0,1},{1,2},{2,3},{3,4},{4,5},{5,6},{6,7},{8,9},{9,10},{10,11},{11... | collective-permute-start | bytes 18488 | tf_op jit(solution)/shard_map/ppermute | solution.py:212
  168.5 21.6 %copy-start.7 = (s32[4,2]{1,0:T(4,128)S(1)}, s32[4,2]{1,0:T(4,128)}, u32[]{:S(2)}) copy-start(s32[4,2]{1,0:T(4,128)} %broadcast_subtract_fusion.place) | copy-start | bytes 100
  184.2 5.9 %collective-permute-start.14 = (f32[2,1,768]{2,1,0:T(1,128)S(1)}, f32[2,1,768]{2,1,0:T(1,128)S(1)}, u32[]{:S(2)}, u32[]{:S(2)}) collective-permute-start(f32[2,1,768]{2,1,0:T(1,128)S(1)} %get-tuple-element.61), channel_id=1, source_target_pairs={{8,0},{16,8},{24,16},{32,24},{40,32},{48,40},{56,48},{64,56},{72,6... | collective-permute-start | bytes 18440 | tf_op jit(solution)/shard_map/ppermute | solution.py:215
  185.5 5.9 %collective-permute-start.15 = (f32[2,1,768]{2,1,0:T(1,128)S(1)}, f32[2,1,768]{2,1,0:T(1,128)S(1)}, u32[]{:S(2)}, u32[]{:S(2)}) collective-permute-start(f32[2,1,768]{2,1,0:T(1,128)S(1)} %get-tuple-element.60), channel_id=1, source_target_pairs={{0,8},{8,16},{16,24},{24,32},{32,40},{40,48},{48,56},{56,64},{64,7... | collective-permute-start | bytes 18440 | tf_op jit(solution)/shard_map/ppermute | solution.py:212
  195.7 11.1 %collective-permute-start.16 = (f32[2,770,1]{1,0,2:T(2,128)S(1)}, f32[2,770,1]{1,0,2:T(2,128)S(1)}, u32[]{:S(2)}, u32[]{:S(2)}) collective-permute-start(f32[2,770,1]{1,0,2:T(2,128)S(1)} %copy.26), channel_id=1, source_target_pairs={{1,0},{2,1},{3,2},{4,3},{5,4},{6,5},{7,6},{9,8},{10,9},{11,10},{12... | collective-permute-start | bytes 18488 | tf_op jit(solution)/shard_map/ppermute | solution.py:215
  198.4 9.6 %collective-permute-start.17 = (f32[2,770,1]{1,0,2:T(2,128)S(1)}, f32[2,770,1]{1,0,2:T(2,128)S(1)}, u32[]{:S(2)}, u32[]{:S(2)}) collective-permute-start(f32[2,770,1]{1,0,2:T(2,128)S(1)} %copy.28), channel_id=1, source_target_pairs={{0,1},{1,2},{2,3},{3,4},{4,5},{5,6},{6,7},{8,9},{9,10},{10,11},{11... | collective-permute-start | bytes 18488 | tf_op jit(solution)/shard_map/ppermute | solution.py:212
  224.0 106.1 %copy-start.3 = (f32[1,6,256,256]{3,1,2,0:T(8,128)S(1)}, f32[1,6,256,256]{3,1,2,0:T(8,128)}, u32[]{:S(2)}) copy-start(f32[1,6,256,256]{3,1,2,0:T(8,128)} %copy.31) | copy-start | bytes 4718596
  226.2 101.4 %collective-permute-start.18 = (f32[2,768,128]{2,1,0:T(8,128)}, f32[2,768,128]{2,1,0:T(8,128)S(1)}, u32[]{:S(2)}, u32[]{:S(2)}) collective-permute-start(f32[2,768,128]{2,1,0:T(8,128)} %slice.267), channel_id=1, source_target_pairs={{1,0},{2,1},{3,2},{4,3},{5,4},{6,5},{7,6},{9,8},{10,9},{11,10},{12... | collective-permute-start | bytes 2359304 | tf_op jit(solution)/shard_map/ppermute | solution.py:204
  325.5 4.6 %copy-start.6 = (f32[7,65536]{1,0:T(8,128)S(1)}, f32[7,65536]{1,0:T(8,128)}, u32[]{:S(2)}) copy-start(f32[7,65536]{1,0:T(8,128)} %all-reduce.2.cloned.1.call-done) | copy-start | bytes 5505028
  328.8 23.9 %collective-permute-start.19 = (f32[2,128,896]{2,1,0:T(8,128)S(1)}, f32[2,128,896]{2,1,0:T(8,128)S(1)}, u32[]{:S(2)}, u32[]{:S(2)}) collective-permute-start(f32[2,128,896]{2,1,0:T(8,128)S(1)} %pad_maximum_fusion.33), channel_id=1, source_target_pairs={{8,0},{16,8},{24,16},{32,24},{40,32},{48,40},{56,48},{64,56},{72,6... | collective-permute-start | bytes 2752520 | tf_op jit(solution)/shard_map/ppermute | solution.py:204
  (1 other events, 1.8 us)
Sparse Core Ops, SparseCore 0:
  166.3 159.2 all-reduce.1
where the time goes:
time: 384 us; the launch traced here: 381 us
  waiting for transfers between devices  133 us (35%)
  starting transfers between devices  78.5 us (20%)
  other arithmetic  70.4 us (18%)
  local copies, waits for them, and re-layouts  55.9 us (15%)
  Pallas kernels  28.9 us (8%)
  between operations  14.5 us (4%)
    psum x1, waiting for transfers between devices, per_device(): totals = lax.psum(packed, ('row', 'col'))  98 us
    ppermute x8, starting transfers between devices, extended_2(): lax.ppermute(lax.slice_in_dim(block, block.shape[dim] - width, None, axis...  59.8 us
    div x5, other arithmetic, per_device(): field = (rhs + smooth_weight * neighbours(padded)) / diagonal  50.2 us
    pallas_call x1, Pallas kernels, frames(): pl.pallas_call(frame_kernel, grid_spec=grid, out_shape=[jax.ShapeDtypeStr...  28.9 us
    ppermute x4, waiting for transfers between devices, from_behind(): return lax.ppermute(block, axis, route)  23.3 us
    gather x12, local copies, waits for them, and re-layouts  16.4 us
    ppermute x8, waiting for transfers between devices, extended_2(): lax.ppermute(lax.slice_in_dim(block, block.shape[dim] - width, None, axis...  11.9 us
    ppermute x8, starting transfers between devices, extended_2(): lax.ppermute(lax.slice_in_dim(block, 0, width, axis=dim), axis, backward)  10.3 us
  transfers between devices with their start and end apart: 21, of which 7 were waited for; matrix products, arithmetic and copies ran while one was open for 17% of the time, Pallas kernels for 0%

commit v1 on v0

--- a/solution.py
+++ b/solution.py
@@ -13,6 +13,11 @@
 MODES = 3
 TILE = 768
 WIDE = TILE + H
+TILES = 8
+ROWS = 904
+BAND = 136
+LOW = TILE - 8
+MESH = pl.DeviceIdType.MESH
 F32, BF16 = jnp.float32, jnp.bfloat16
 
 
@@ -103,13 +108,14 @@
     return xr, xi
 
 
-def frame_kernel(place, amp, patches, dual, probe, tab, order, dual_new, canvas, sums, far):
+def frame_kernel(place, amp, patches, dual, probe, tab, order, dual_new, canvas, sums, count, far):
     f = pl.program_id(0)
 
     @pl.when(f == 0)
     def _():
         canvas[...] = jnp.zeros_like(canvas)
         sums[...] = jnp.zeros_like(sums)
+        count[...] = jnp.zeros_like(count)
 
     pr, pi = patches[0, 0], patches[0, 1]
     sums[6] += pr * pr + pi * pi
@@ -148,11 +154,13 @@
         obj_re = re if obj_re is None else obj_re + re
         obj_im = im if obj_im is None else obj_im + im
     r = pl.multiple_of(place[f, 0], H)
-    c = pl.multiple_of(place[f, 1], H)
-    canvas[0, pl.ds(r, N), pl.ds(c, N)] += obj_re
-    canvas[1, pl.ds(r, N), pl.ds(c, N)] += obj_im
-    square = probe[...] * probe[...]
-    canvas[2, pl.ds(r, N), pl.ds(c, N)] += jnp.sum(square, axis=(0, 1))
+    c = place[f, 1] // H
+    for p, value in enumerate((obj_re, obj_im)):
+        canvas[p, c, pl.ds(r, N)] += lft(value)
+        canvas[p, c + 1, pl.ds(r, N)] += rgt(value)
+    line = lax.broadcasted_iota(jnp.int32, (8, H), 0)
+    lane = lax.broadcasted_iota(jnp.int32, (8, H), 1)
+    count[...] += jnp.where((line == place[f, 0] // H) & (lane == c), 1.0, 0.0)
 
 
 def frames(place, amp, patches, dual, probe):
@@ -172,8 +180,9 @@
         ],
         out_specs=[
             pl.BlockSpec((1, MODES, 2, N, N), lambda f, p: (f, 0, 0, 0, 0)),
-            whole(3, WIDE, WIDE),
+            whole(2, TILES, ROWS, H),
             whole(7, N, N),
+            whole(8, H),
         ],
         scratch_shapes=[pltpu.VMEM((MODES, 2, N, N), F32)],
     )
@@ -182,85 +191,363 @@
         grid_spec=grid,
         out_shape=[
             jax.ShapeDtypeStruct(dual.shape, F32),
-            jax.ShapeDtypeStruct((3, WIDE, WIDE), F32),
+            jax.ShapeDtypeStruct((2, TILES, ROWS, H), F32),
             jax.ShapeDtypeStruct((7, N, N), F32),
+            jax.ShapeDtypeStruct((8, H), F32),
         ],
         compiler_params=pltpu.CompilerParams(vmem_limit_bytes=56 << 20),
     )(place, amp, patches, dual, probe, tab, order)
 
 
-SWEEPS = 4
-
-
-amp_floor = 1.0
-obj_weight = 0.5
-smooth_weight = 16.0
-probe_weight = 1.0
-
-
-def from_behind(block, axis, distance):
-    devices = range(lax.axis_size(axis))
-    route = [(i - distance, i) for i in devices if i - distance in devices]
-    return lax.ppermute(block, axis, route)
-
-
-def extended_2(block, sides, width):
-    for axis, dim in sides:
-        count = lax.axis_size(axis)
-        forward = [(i, i + 1) for i in range(count - 1)]
-        backward = [(target, source) for source, target in forward]
-        low = lax.ppermute(
-            lax.slice_in_dim(block, block.shape[dim] - width, None, axis=dim), axis, forward
+def exchange_kernel(canvas, obj, sums, probe, count, cl, cr, bu, bd, ol, orr, ou, od, window, probe_new,
+                    band_t, band_b, oband_t, oband_b, pair_in, half, y_in, quarter, x_in, chunk, z_all,
+                    cnt_l, cnt_r, cnt_a, cnt_u, cnt_d, load_sem, send_sem, recv_sem):
+    i, j = lax.axis_index("row"), lax.axis_index("col")
+    y, z, x, core = i // 4, i % 4, j // 2, j % 2
+    up, down = ((i + 15) % 16, j), ((i + 1) % 16, j)
+    lf, rt = (i, (j + 7) % 8), (i, (j + 1) % 8)
+    twin = (i, x * 2 + 1 - core)
+    ys = [(((y + d) % 4) * 4 + z, j) for d in (1, 2, 3)]
+    xs = [(i, ((x + d) % 4) * 2 + core) for d in (1, 2, 3)]
+    zs = [(y * 4 + (z + d) % 4, j) for d in (1, 2, 3)]
+    peers = [up, down, lf, rt, twin] + ys + xs + zs
+
+    loads = [
+        pltpu.make_async_copy(canvas.at[:, :, pl.ds(0, BAND)], band_t, load_sem.at[0]),
+        pltpu.make_async_copy(canvas.at[:, :, pl.ds(LOW, BAND)], band_b, load_sem.at[1]),
+    ]
+    for t in range(6):
+        lanes = pl.ds(H * t, H)
+        loads.append(pltpu.make_async_copy(obj.at[:, pl.ds(0, BAND), lanes], oband_t.at[:, t], load_sem.at[2 + t]))
+        loads.append(pltpu.make_async_copy(obj.at[:, pl.ds(LOW, 8), lanes], oband_b.at[:, t], load_sem.at[8 + t]))
+    for c in loads:
+        c.start()
+
+    barrier = pltpu.get_barrier_semaphore()
+    for p in peers:
+        pl.semaphore_signal(barrier, inc=1, device_id=p, device_id_type=MESH)
+    pl.semaphore_wait(barrier, len(peers))
+
+    used = [0]
+    started = []
+
+    def send(src, dst, to):
+        k = used[0]
+        used[0] += 1
+        c = pltpu.make_async_remote_copy(
+            src_ref=src, dst_ref=dst, send_sem=send_sem.at[k], recv_sem=recv_sem.at[k],
+            device_id=to, device_id_type=MESH,
         )
-        high = lax.ppermute(lax.slice_in_dim(block, 0, width, axis=dim), axis, backward)
-        block = jnp.concatenate([low, block, high], axis=dim)
-    return block
-
-
-def neighbours(padded):
-    return padded[:, 2:, 1:-1] + padded[:, :-2, 1:-1] + padded[:, 1:-1, 2:] + padded[:, 1:-1, :-2]
+        c.start()
+        started.append(c)
+        return c
+
+    def landed(*copies):
+        for c in copies:
+            c.wait_recv()
+
+    other = pl.ds(pl.multiple_of((1 - core) * H, H), H)
+    mine = pl.ds(pl.multiple_of(core * H, H), H)
+    a_pair = send(sums.at[:, other], pair_in, twin)
+
+    cols = []
+    for r, n in ((0, BAND), (LOW, BAND)):
+        rows = pl.ds(r, n)
+        cols.append(send(canvas.at[:, pl.ds(5, 2), rows], cl.at[:, :, rows], rt))
+        cols.append(send(canvas.at[:, pl.ds(0, 2), rows], cr.at[:, :, rows], lf))
+    for r, n in ((0, BAND), (LOW, 8)):
+        rows = pl.ds(r, n)
+        cols.append(send(obj.at[:, rows, pl.ds(5 * H, H)], ol.at[:, rows], rt))
+        cols.append(send(obj.at[:, rows, pl.ds(0, H)], orr.at[:, 0, rows], lf))
+        cols.append(send(obj.at[:, rows, pl.ds(H, H)], orr.at[:, 1, rows], lf))
+    cols.append(send(count, cnt_l, rt))
+    cols.append(send(count, cnt_r, lf))
+
+    landed(a_pair)
+    half[...] = sums[:, mine] + pair_in[...]
+    a_y = []
+    for d in (1, 2, 3):
+        rows = pl.ds(pl.multiple_of(((y + d) % 4) * 32, 32), 32)
+        a_y.append(send(half.at[:, rows], y_in.at[d - 1], ys[d - 1]))
+
+    landed(*cols)
+    for c in loads:
+        c.wait()
+    lane = lax.broadcasted_iota(jnp.int32, (1, 8, H), 2)
+
+    def edge(from_right, from_left):
+        return jnp.where(lane < 4, from_right, jnp.where(lane >= H - 4, from_left, 0.0))
+
+    def widen(first, band, oband, orows):
+        def step(g, carry):
+            at, src = pl.ds(pl.multiple_of(g * 8, 8), 8), pl.ds(pl.multiple_of(first + g * 8, 8), 8)
+            band[:, 0, at] += cl[:, 1, src]
+            band[:, 6, at] += cr[:, 0, src]
+            band[:, 7, at] = edge(cr[:, 1, src], cl[:, 0, src])
+            return carry
+
+        def ostep(g, carry):
+            at, src = pl.ds(pl.multiple_of(g * 8, 8), 8), pl.ds(pl.multiple_of(first + g * 8, 8), 8)
+            oband[:, 6, at] = orr[:, 0, src]
+            oband[:, 7, at] = edge(orr[:, 1, src], ol[:, src])
+            return carry
+
+        lax.fori_loop(0, BAND // 8, step, 0)
+        lax.fori_loop(0, orows // 8, ostep, 0)
+
+    widen(0, band_t, oband_t, BAND)
+    widen(LOW, band_b, oband_b, 8)
+    lane2 = lax.broadcasted_iota(jnp.int32, (8, H), 1)
+    cnt_a[...] = jnp.where(
+        lane2 < 2, pltpu.roll(cnt_l[...], H - 4, 1),
+        jnp.where(lane2 < 8, pltpu.roll(count[...], 2, 1), jnp.where(lane2 < 10, pltpu.roll(cnt_r[...], 8, 1), 0.0)),
+    )
+    rows_ = [
+        send(band_t, bd, up),
+        send(band_b, bu, down),
+        send(cnt_a, cnt_d, up),
+        send(cnt_a, cnt_u, down),
+        send(oband_t, od, up),
+        send(oband_b, ou, down),
+    ]
+    rest = pl.ds(BAND, LOW - BAND)
+    rows_ += [
+        send(canvas.at[:, pl.ds(5, 2), rest], cl.at[:, :, rest], rt),
+        send(canvas.at[:, pl.ds(0, 2), rest], cr.at[:, :, rest], lf),
+        send(obj.at[:, rest, pl.ds(5 * H, H)], ol.at[:, rest], rt),
+        send(obj.at[:, rest, pl.ds(0, H)], orr.at[:, 0, rest], lf),
+        send(obj.at[:, rest, pl.ds(H, H)], orr.at[:, 1, rest], lf),
+    ]
+
+    landed(*a_y)
+    rows = pl.ds(pl.multiple_of(y * 32, 32), 32)
+    quarter[...] = half[:, rows] + y_in[0] + y_in[1] + y_in[2]
+    a_x = []
+    for d in (1, 2, 3):
+        rows = pl.ds(pl.multiple_of(((x + d) % 4) * 8, 8), 8)
+        a_x.append(send(quarter.at[:, rows], x_in.at[d - 1], xs[d - 1]))
+    landed(*a_x)
+    rows = pl.ds(pl.multiple_of(x * 8, 8), 8)
+    chunk[...] = quarter[:, rows] + x_in[0] + x_in[1] + x_in[2]
+    z_all[pl.ds(z, 1)] = chunk[...][None]
+    a_z = [send(chunk, z_all.at[z], to) for to in zs]
+    landed(*a_z)
+    total = z_all[0] + z_all[1] + z_all[2] + z_all[3]
+    at8 = pl.ds(pl.multiple_of(core * H + y * 32 + x * 8, 8), 8)
+    at32 = pl.ds(pl.multiple_of(core * H + y * 32, 32), 32)
+    probe_new[:, at8] = (total[:6] + probe[:, at8]) / (total[6:] + 1.0)
+    landed(*[send(probe_new.at[:, at8], probe_new.at[:, at8], to) for to in xs])
+    landed(*[send(probe_new.at[:, at32], probe_new.at[:, at32], to) for to in ys])
+    at128 = pl.ds(pl.multiple_of(core * H, H), H)
+    landed(send(probe_new.at[:, at128], probe_new.at[:, at128], twin))
+
+    landed(*rows_)
+    line = lax.broadcasted_iota(jnp.int32, (8, H), 0)
+    above, own, below = pltpu.roll(cnt_u[...], 4, 0), pltpu.roll(cnt_a[...], 2, 0), cnt_d[...]
+    window[pl.ds(0, 8)] = jnp.where(line < 2, above, own)
+    window[pl.ds(8, 8)] = jnp.where(line < 2, below, 0.0)
+    for c in started:
+        c.wait_send()
+
+
+def exchange(canvas, obj, sums, probe, count):
+    f32 = lambda *d: jax.ShapeDtypeStruct(d, F32)
+    vm, any_ = pl.BlockSpec(memory_space=pltpu.VMEM), pl.BlockSpec(memory_space=pl.ANY)
+    v = lambda *d: pltpu.VMEM(d, F32)
+    return pl.pallas_call(
+        exchange_kernel,
+        out_shape=[
+            f32(2, 2, WIDE, H), f32(2, 2, WIDE, H), f32(2, TILES, BAND, H), f32(2, TILES, BAND, H),
+            f32(2, TILE, H), f32(2, 2, TILE, H), f32(2, TILES, 8, H), f32(2, TILES, BAND, H),
+            f32(16, H), f32(6, N, N),
+        ],
+        in_specs=[any_, any_, vm, vm, vm],
+        out_specs=[vm] * 10,
+        scratch_shapes=[
+            v(2, TILES, BAND, H), v(2, TILES, BAND, H), v(2, TILES, BAND, H), v(2, TILES, 8, H),
+            v(7, H, N), v(7, H, N), v(3, 7, 32, N), v(7, 32, N), v(3, 7, 8, N), v(7, 8, N), v(4, 7, 8, N),
+            v(8, H), v(8, H), v(8, H), v(8, H), v(8, H),
+            pltpu.SemaphoreType.DMA((14,)), pltpu.SemaphoreType.DMA((48,)), pltpu.SemaphoreType.DMA((48,)),
+        ],
+        compiler_params=pltpu.CompilerParams(
+            collective_id=1, has_side_effects=True, vmem_limit_bytes=48 << 20
+        ),
+        cost_estimate=pl.CostEstimate(flops=10**6, bytes_accessed=40 * 10**6, transcendentals=0),
+    )(canvas, obj, sums, probe, count)
+
+
+STRIDE = ROWS // 8
+
+
+def sweep_kernel(spot, place, canvas, obj, cl, cr, bu, bd, ol, orr, ou, od, window, probe,
+                 object_new, patches_new, f0, f1, rhs, wgt, cnt, pwr, sems):
+    i, j = spot[0], spot[1]
+    copies = [
+        pltpu.make_async_copy(canvas, rhs, sems.at[0]),
+        pltpu.make_async_copy(od, f0.at[:, :, pl.ds(TILE, BAND)], sems.at[1]),
+        pltpu.make_async_copy(orr, f0.at[:, pl.ds(6, 2), pl.ds(0, TILE)], sems.at[2]),
+    ]
+    for t in range(6):
+        copies.append(pltpu.make_async_copy(
+            obj.at[:, :, pl.ds(H * t, H)], f0.at[:, t, pl.ds(0, TILE)], sems.at[3 + t]))
+    for c in copies:
+        c.start()
+
+    power = None
+    for m in range(MODES):
+        for p in range(2):
+            q = probe[m, p]
+            power = q * q if power is None else power + q * q
+    for a in range(2):
+        for b in range(2):
+            pwr[a, b] = power[a * H:(a + 1) * H, b * H:(b + 1) * H].reshape(16, 8, H)
+    lanes = lax.broadcasted_iota(jnp.int32, (H, TILES * H), 1)
+    slot = lax.broadcasted_iota(jnp.int32, (H, TILES * H), 0)
+    block = jnp.where(lanes >= 7 * H + H // 2, -1, lanes // H)
+    for b in range(2):
+        pick = jnp.where(slot == block - b + 2, 1.0, 0.0).astype(BF16)
+        wide = dot(window[...].astype(BF16), pick)
+        for r in range(10):
+            line = jnp.broadcast_to(wide[r:r + 1], (8, TILES * H))
+            for t in range(TILES):
+                cnt[b, r, t] = line[:, t * H:(t + 1) * H]
+    for c in copies:
+        c.wait()
+
+    tile = lax.broadcasted_iota(jnp.int32, (TILES, 8, H), 0)
+    sub = lax.broadcasted_iota(jnp.int32, (TILES, 8, H), 1)
+    lane = lax.broadcasted_iota(jnp.int32, (TILES, 8, H), 2)
+    col = jnp.where(tile < 7, tile * H + lane, jnp.where(lane < H // 2, 7 * H + lane, lane - H))
+    col = col + j * TILE
+    col_ok = (col >= 0) & (col < 8 * TILE) & ((tile < 7) | (lane < 4) | (lane >= H - 4))
+    lane1 = lax.broadcasted_iota(jnp.int32, (8, H), 1)
+    sub1 = lax.broadcasted_iota(jnp.int32, (8, H), 0)
+
+    def finish(at, den, ok, extra):
+        inv = jnp.where(ok, 1.0 / (den + (0.5 + 4.0 * 16.0)), 0.0)
+        wgt[:, at] = 16.0 * inv
+        for p in range(2):
+            field = jnp.where(ok, f0[p, :, at], 0.0)
+            f0[p, :, at] = field
+            rhs[p, :, at] = (rhs[p, :, at] + extra[p] + 0.5 * field) * inv
+
+    for r in range(7):
+        def step(g, carry, r=r):
+            row = r * H + g * 8
+            at = pl.ds(pl.multiple_of(row, 8), 8)
+            den = None
+            for a in range(2):
+                for b in range(2):
+                    term = cnt[b, r - a + 2] * pwr[a, b, g][None]
+                    den = term if den is None else den + term
+            ok = col_ok & (i * TILE + row < 16 * TILE)
+            extra = []
+            for p in range(2):
+                rhs[p, 0, at] += cl[p, 1, at]
+                rhs[p, 6, at] += cr[p, 0, at]
+                rhs[p, 7, at] = jnp.where(lane1 < 4, cr[p, 1, at], jnp.where(lane1 >= H - 4, cl[p, 0, at], 0.0))
+                if r < 6:
+                    f0[p, 7, at] = jnp.where(lane1 < 4, f0[p, 7, at], ol[p, at])
+                if r == 0:
+                    extra.append(bu[p, :, pl.ds(pl.multiple_of(g * 8 + 8, 8), 8)])
+                elif r == 6:
+                    extra.append(bd[p, :, pl.ds(pl.multiple_of(g * 8, 8), 8)])
+                else:
+                    extra.append(0.0)
+            finish(at, den, ok, extra)
+            return carry
+
+        lax.fori_loop(0, 16, step, 0)
+
+    at = pl.ds(7 * H, 8)
+    den = None
+    for a in range(2):
+        for b in range(2):
+            low = cnt[b, 7 - a + 2] * pwr[a, b, 0][None]
+            high = cnt[b, -1 - a + 2] * pwr[a, b, 15][None]
+            term = jnp.where(sub < 4, low, high)
+            den = term if den is None else den + term
+    row_ok = ((sub < 4) & (i < 15)) | ((sub >= 4) & (i > 0))
+    extra = []
+    for p in range(2):
+        rhs[p, :, at] = jnp.zeros((TILES, 8, H), F32)
+        extra.append(jnp.where(sub < 4, bd[p, :, pl.ds(H, 8)], bu[p, :, pl.ds(0, 8)]))
+        f0[p, :, at] = jnp.where(sub < 4, f0[p, :, at], ou[p])
+    finish(at, den, col_ok & row_ok, extra)
+
+    def sweep(src, dst):
+        for p in range(2):
+            rows = lambda t: (p, slice(None), pl.ds(t, 8, stride=STRIDE), slice(None))
+
+            def update(t, above, here, below):
+                west = jnp.concatenate([here[7:], here[:7]], axis=0)
+                east = jnp.concatenate([here[1:], here[:1]], axis=0)
+                west = pltpu.roll(jnp.where(lane == H - 1, west, here), 1, 2)
+                east = pltpu.roll(jnp.where(lane == 0, east, here), H - 1, 2)
+                near = (above + below) + (west + east)
+                w = wgt[:, pl.ds(t, 8, stride=STRIDE), :]
+                dst[rows(t)] = rhs[rows(t)] + w * near
+
+            first, last = src[rows(0)], src[rows(STRIDE - 1)]
+
+            def step(t, carry):
+                above, here = carry
+                below = src[rows(t + 1)]
+                update(t, above, here, below)
+                return here, below
+
+            above, here = lax.fori_loop(0, STRIDE - 1, step, (pltpu.roll(last, 1, 1), first), unroll=4)
+            update(STRIDE - 1, above, here, pltpu.roll(first, 7, 1))
+
+    sweep(f0, f1)
+    sweep(f1, f0)
+    sweep(f0, f1)
+    sweep(f1, f0)
+
+    outs = []
+    for t in range(6):
+        outs.append(pltpu.make_async_copy(
+            f0.at[:, t, pl.ds(0, TILE)], object_new.at[:, :, pl.ds(H * t, H)], sems.at[t]))
+    for f in range(place.shape[0]):
+        r = pl.multiple_of(place[f, 0], H)
+        for t in range(2):
+            outs.append(pltpu.make_async_copy(
+                f0.at[:, place[f, 1] // H + t, pl.ds(r, N)],
+                patches_new.at[f, :, :, pl.ds(H * t, H)], sems.at[6 + 2 * f + t]))
+    for c in outs:
+        c.start()
+    for c in outs:
+        c.wait()
+
+
+def sweeps(spot, place, canvas, obj, cl, cr, bu, bd, ol, orr, ou, od, window, probe):
+    vm, any_ = pl.BlockSpec(memory_space=pltpu.VMEM), pl.BlockSpec(memory_space=pl.ANY)
+    sm = pl.BlockSpec(memory_space=pltpu.SMEM)
+    v = lambda *d: pltpu.VMEM(d, F32)
+    return pl.pallas_call(
+        sweep_kernel,
+        out_shape=[
+            jax.ShapeDtypeStruct(obj.shape, F32),
+            jax.ShapeDtypeStruct((place.shape[0], 2, N, N), F32),
+        ],
+        in_specs=[sm, sm, any_, any_, vm, vm, vm, vm, vm, any_, vm, any_, vm, vm],
+        out_specs=[any_, any_],
+        scratch_shapes=[
+            v(2, TILES, ROWS, H), v(2, TILES, ROWS, H), v(2, TILES, ROWS, H), v(TILES, ROWS, H),
+            v(2, 10, TILES, 8, H), v(2, 2, 16, 8, H), pltpu.SemaphoreType.DMA((16,)),
+        ],
+        compiler_params=pltpu.CompilerParams(vmem_limit_bytes=60 << 20),
+    )(spot, place, canvas, obj, cl, cr, bu, bd, ol, orr, ou, od, window, probe)
 
 
 def per_device(amplitude, patches, dual, probe, obj, positions):
-    width = amplitude.shape[-1]
-    half_width = width // 2
-    modes = probe.shape[0]
-    tile = obj.shape[1]
-    row_index = lax.axis_index("row")
-    col_index = lax.axis_index("col")
-    origin = jnp.stack([row_index, col_index]).astype(jnp.int32) * tile
-    place = positions - origin
-    dual_new, canvas, sums = frames(place, amplitude, patches, dual, probe)
-    packed = sums.reshape(7, width * width)
-    probe_flat = probe.reshape(2 * modes, width * width)
-    totals = lax.psum(packed, ("row", "col"))
-    probe_new = (
-        (totals[: 2 * modes] + probe_weight * probe_flat) / (totals[2 * modes :] + probe_weight)
-    ).reshape(probe.shape)
-    local_rows = place[:, 0]
-    local_cols = place[:, 1]
-    anchor = jnp.zeros((), jnp.int32)
-
-    from_left = from_behind(canvas[:, :, tile:], "col", 1)
-    canvas = canvas.at[:, :, :half_width].add(from_left)
-    from_above = from_behind(canvas[:, tile:, :tile], "row", 1)
-    sums_own = canvas[:, :tile, :tile].at[:, :half_width, :].add(from_above)
-    rhs = sums_own[:2] + obj_weight * obj
-    diagonal = sums_own[2] + obj_weight + 4.0 * smooth_weight
-    field = obj
-    for sweep in range(SWEEPS):
-        padded = extended_2(field, (("row", 1), ("col", 2)), 1)
-        field = (rhs + smooth_weight * neighbours(padded)) / diagonal
-    from_right = from_behind(field[:, :, :half_width], "col", -1)
-    wider = jnp.concatenate([field, from_right], axis=2)
-    from_below = from_behind(wider[:, :half_width, :], "row", -1)
-    extended = jnp.concatenate([wider, from_below], axis=1)
-
-    def window(row_start, col_start):
-        return lax.dynamic_slice(extended, (anchor, row_start, col_start), (2, width, width))
-
-    patches_new = jax.vmap(window)(local_rows, local_cols)
-    return (dual_new, field, probe_new, patches_new)
+    spot = jnp.stack([lax.axis_index("row"), lax.axis_index("col")]).astype(jnp.int32)
+    place = positions - spot * TILE
+    dual_new, canvas, sums, count = frames(place, amplitude, patches, dual, probe)
+    cl, cr, bu, bd, ol, orr, ou, od, window, probe_new = exchange(
+        canvas, obj, sums, probe.reshape(2 * MODES, N, N), count)
+    object_new, patches_new = sweeps(spot, place, canvas, obj, cl, cr, bu, bd, ol, orr, ou, od, window, probe)
+    return dual_new, object_new, probe_new.reshape(probe.shape), patches_new
 
 
 def solution(mesh):

time: 384 us -> 179 us (0.47)
  the two profiles are of different devices: /device:TPU:0 before, /device:TPU:97 now
where the time goes in v1:
time: 179 us
  Pallas kernels  168 us (94%)
  local copies, waits for them, and re-layouts  8.92 us (5%)
    pallas_call x1, Pallas kernels, exchange(): pl.pallas_call(exchange_kernel, out_shape=[f32(2, 2, WIDE, H), f32(2, 2,...  94.1 us
    pallas_call x1, Pallas kernels, sweeps(): pl.pallas_call(sweep_kernel, out_shape=[jax.ShapeDtypeStruct(obj.shape, F...  46.6 us
    pallas_call x1, Pallas kernels, frames(): pl.pallas_call(frame_kernel, grid_spec=grid, out_shape=[jax.ShapeDtypeStr...  27.3 us
    unnamed x20, local copies, waits for them, and re-layouts  8.92 us

profile of v1, /device:TPU:97, one launch (start us, length us, event | category | flops | bytes accessed | tf_op | source)
XLA Modules:
  0.0 178.7 jit_solution(18386879589854655478)
XLA Ops:
  0.6 0.6 broadcast_multiply_fusion
  1.2 0.8 copy.12
  2.0 0.6 broadcast_subtract_fusion.place
  2.5 27.3 %shard_map.111 = (f32[4,3,2,256,256]{4,3,2,1,0:T(8,128)}, f32[2,8,904,128]{3,2,1,0:T(8,128)}, f32[7,256,256]{2,1,0:T(8,128)}, f32[8,128]{1,0:T(8,128)}) custom-call(s32[4,2]{1,0:T(4,128)} %broadcast_subtract_fusion.place, f32[4,256,256]{2,1,0:T(8,128)} %amp.1, f32[4,2,256,256]{3,2,1,0:T(8,128)} %patches.1, f32[4,3,2,256,256]{4,3,2,1,0:T(8,128)} %dual.1, ...), custom_call_target="tpu_custom_call" | custom-call | tf_op jit(solution)/shard_map/pallas_call | solution.py:189
  29.8 0.0 copy-start.7
  29.8 0.7 copy-done.7
  30.5 94.1 %shard_map.112 = (f32[2,2,896,128]{3,2,1,0:T(8,128)}, f32[2,2,896,128]{3,2,1,0:T(8,128)}, f32[2,8,136,128]{3,2,1,0:T(8,128)S(1)}, f32[2,8,136,128]{3,2,1,0:T(8,1...) custom-call(f32[2,8,904,128]{3,2,1,0:T(8,128)} %get-tuple-element.21, ...), custom_call_target="tpu_custom_call" | custom-call | flops 1000000 | bytes 40000000 | tf_op jit(solution)/shard_map/pallas_call | solution.py:357
  124.6 0.0 copy-start
  124.7 1.1 copy-done
  125.8 0.0 copy-start.1
  125.8 1.0 copy-done.1
  126.8 0.0 copy-start.2
  126.8 1.0 copy-done.2
  127.8 0.0 copy-start.3
  127.8 1.0 copy-done.3
  128.9 0.0 copy-start.4
  128.9 0.9 copy-done.4
  129.8 0.0 copy-start.5
  129.8 0.6 copy-done.5
  130.4 0.0 copy-start.6
  130.4 0.6 copy-done.6
  131.0 0.0 copy-start.8
  131.0 46.6 %shard_map.113 = (f32[2,768,768]{2,1,0:T(8,128)}, f32[4,2,256,256]{3,2,1,0:T(8,128)}) custom-call(s32[2]{0:T(128)} %get-tuple-element.37.spot, s32[4,2]{1,0:T(4,128)} %broadcast_subtract_fusion.place, f32[2,8,904,128]{3,2,1,0:T(8,128)} %get-tuple-element.21.canvas, f32[2,768,768]{2,1,0:T(8,128)} %obj.3, f32[2,2,896,128]{3,2,1,0:T(8,128)} %get-tuple-element.24.cl, ...), custom_call_target="tpu_custom_call" | custom-call | tf_op jit(solution)/shard_map/pallas_call | solution.py:527
  177.6 0.0 copy-done.8
  177.6 1.1 copy.14
Async XLA Ops:
  29.8 0.7 copy-start.7
  124.6 1.1 copy-start
  125.8 1.0 copy-start.1
  126.8 1.0 copy-start.2
  127.8 1.0 copy-start.3
  128.9 0.9 copy-start.4
  129.8 0.6 copy-start.5
  130.4 0.6 copy-start.6
  131.0 46.6 %copy-start.8 = (f32[6,256,256]{2,1,0:T(8,128)S(1)}, f32[6,256,256]{2,1,0:T(8,128)}, u32[]{:S(2)}) copy-start(f32[6,256,256]{2,1,0:T(8,128)} %get-tuple-element.34) | copy-start | bytes 4718596

commit v2 on v0

v2 whole, which is shorter than its diff:
```python
import math
import numpy as np
import ml_dtypes
import jax
import jax.numpy as jnp
from jax import lax
from jax.experimental import pallas as pl
from jax.experimental.pallas import tpu as pltpu
from jax.sharding import PartitionSpec as P

N = 256
H = 128
MODES = 3
TILE = 768
WIDE = TILE + H
TILES = 8
ROWS = 904
BAND = 136
LOW = TILE - 8
MESH = pl.DeviceIdType.MESH
F32, BF16 = jnp.float32, jnp.bfloat16


def dft_tables():
    k = np.arange(H)
    stacked = []
    for odd in (0, 1):
        angle = ((2 * k[:, None] + odd) * k[None, :] % N) * (2.0 * math.pi / N)
        c, s = np.cos(angle) / 16.0, np.sin(angle) / 16.0
        stacked.append(np.block([[c, s], [-s, c]]))
    whole = np.stack(stacked + [t.T for t in stacked]).astype(np.float32)
    lead = whole.astype(ml_dtypes.bfloat16)
    rest = (whole - lead.astype(np.float32)).astype(ml_dtypes.bfloat16)
    return np.stack([lead, rest], axis=1)


def order_table():
    t = np.zeros((N, N), np.float32)
    k = np.arange(H)
    t[2 * k, k] = 1.0
    t[2 * k + 1, H + k] = 1.0
    return np.stack([t, t.T]).astype(ml_dtypes.bfloat16)


def parts(x):
    lead = x.astype(BF16)
    return lead, (x - lead.astype(F32)).astype(BF16)


def dot(a, b):
    return lax.dot_general(a, b, (((1,), (0,)), ((), ())), preferred_element_type=F32)


def left(tab, which, x):
    lead, rest = parts(x)
    a, b = tab[which, 0], tab[which, 1]
    return dot(jnp.concatenate([a, a, b], axis=1), jnp.concatenate([lead, rest, lead], axis=0))


def right(tab, which, x):
    lead, rest = parts(x)
    a, b = tab[which, 0], tab[which, 1]
    return dot(jnp.concatenate([lead, rest, lead], axis=1), jnp.concatenate([a, a, b], axis=0))


def top(x):
    return x[:H]


def bot(x):
    return x[H:]


def lft(x):
    return x[:, :H]


def rgt(x):
    return x[:, H:]


def rows2(a, b):
    return jnp.concatenate([a, b], axis=0)


def cols2(a, b):
    return jnp.concatenate([a, b], axis=1)


def forward(tab, xr, xi):
    e = left(tab, 0, rows2(top(xr) + bot(xr), top(xi) + bot(xi)))
    o = left(tab, 1, rows2(top(xr) - bot(xr), top(xi) - bot(xi)))
    yr, yi = rows2(top(e), top(o)), rows2(bot(e), bot(o))
    even = right(tab, 2, cols2(lft(yr) + rgt(yr), lft(yi) + rgt(yi)))
    odd = right(tab, 3, cols2(lft(yr) - rgt(yr), lft(yi) - rgt(yi)))
    return even, odd


def inverse(tab, even, odd):
    a = right(tab, 0, even)
    b = right(tab, 1, odd)
    yr = cols2(lft(a) + lft(b), lft(a) - lft(b))
    yi = cols2(rgt(a) + rgt(b), rgt(a) - rgt(b))
    e = left(tab, 2, rows2(top(yr), top(yi)))
    o = left(tab, 3, rows2(bot(yr), bot(yi)))
    xr = rows2(top(e) + top(o), top(e) - top(o))
    xi = rows2(bot(e) + bot(o), bot(e) - bot(o))
    return xr, xi


def obj_exchange(f, obj, east, below, west, above, ends_r, ends_l, band_t, band_b, load_sem, send_sem, recv_sem):
    i, j = lax.axis_index("row"), lax.axis_index("col")
    up, down = ((i + 15) % 16, j), ((i + 1) % 16, j)
    lf, rt = (i, (j + 7) % 8), (i, (j + 1) % 8)
    first, last = pl.ds(0, BAND), pl.ds(LOW, 8)

    def remote(k, src, dst, to):
        return pltpu.make_async_remote_copy(
            src_ref=src, dst_ref=dst, send_sem=send_sem.at[k], recv_sem=recv_sem.at[k],
            device_id=to, device_id_type=MESH,
        )

    loads = []
    for t in range(6):
        lanes = pl.ds(H * t, H)
        loads.append(pltpu.make_async_copy(obj.at[:, first, lanes], band_t.at[:, t], load_sem.at[t]))
        loads.append(pltpu.make_async_copy(obj.at[:, last, lanes], band_b.at[:, t], load_sem.at[6 + t]))
    ends = []
    for n, (rows, at) in enumerate(((first, pl.ds(0, BAND)), (last, pl.ds(BAND, 8)))):
        ends.append(remote(3 * n, obj.at[:, rows, pl.ds(0, H)], ends_r.at[:, 0, at], lf))
        ends.append(remote(3 * n + 1, obj.at[:, rows, pl.ds(H, H)], ends_r.at[:, 1, at], lf))
        ends.append(remote(3 * n + 2, obj.at[:, rows, pl.ds(5 * H, H)], ends_l.at[:, at], rt))
    inner, outer = pl.ds(0, 6), pl.ds(6, 2)
    bands_in = [
        remote(6, band_t.at[:, inner], below.at[:, inner], up),
        remote(7, band_b.at[:, inner], above.at[:, inner], down),
    ]
    bands_out = [
        remote(11, band_t.at[:, outer], below.at[:, outer], up),
        remote(12, band_b.at[:, outer], above.at[:, outer], down),
    ]
    sides = [
        remote(8, obj.at[:, :, pl.ds(0, H)], east.at[:, 0], lf),
        remote(9, obj.at[:, :, pl.ds(H, H)], east.at[:, 1], lf),
        remote(10, obj.at[:, :, pl.ds(5 * H, H)], west, rt),
    ]

    @pl.when(f == 0)
    def _():
        barrier = pltpu.get_barrier_semaphore()
        for p in (up, down, lf, rt):
            pl.semaphore_signal(barrier, inc=1, device_id=p, device_id_type=MESH)
        for c in loads:
            c.start()
        pl.semaphore_wait(barrier, 4)
        for c in ends:
            c.start()
        for c in loads:
            c.wait()
        for c in bands_in + sides:
            c.start()

    @pl.when(f == 1)
    def _():
        for c in ends:
            c.wait()
        lane = lax.broadcasted_iota(jnp.int32, (1, 8, H), 2)

        def edge(g, band, to):
            src = pl.ds(pl.multiple_of(g * 8, 8), 8)
            to = pl.ds(pl.multiple_of(to * 8, 8), 8)
            band[:, 6, to] = ends_r[:, 0, src]
            band[:, 7, to] = jnp.where(
                lane < 4, ends_r[:, 1, src], jnp.where(lane >= H - 4, ends_l[:, src], 0.0))

        def step(g, carry):
            edge(g, band_t, g)
            return carry

        lax.fori_loop(0, BAND // 8, step, 0)
        edge(BAND // 8, band_b, 0)
        for c in bands_out:
            c.start()

    return bands_in + sides + bands_out


def frame_kernel(place, amp, patches, dual, probe, tab, order, obj, dual_new, parts_out, sums, count, east, below,
                 west, above, far, *shared):
    f = pl.program_id(0)
    pending = obj_exchange(f, obj, east, below, west, above, *shared)

    @pl.when(f == 0)
    def _():
        sums[...] = jnp.zeros_like(sums)
        count[...] = jnp.zeros_like(count)

    pr, pi = patches[0, 0], patches[0, 1]
    sums[6] += pr * pr + pi * pi
    power_e = power_o = None
    for m in range(MODES):
        qr, qi = probe[m, 0], probe[m, 1]
        xr = qr * pr - qi * pi + dual[0, m, 0]
        xi = qr * pi + qi * pr + dual[0, m, 1]
        even, odd = forward(tab, xr, xi)
        far[m, 0] = even
        far[m, 1] = odd
        e2 = lft(even) * lft(even) + rgt(even) * rgt(even)
        o2 = lft(odd) * lft(odd) + rgt(odd) * rgt(odd)
        power_e = e2 if power_e is None else power_e + e2
        power_o = o2 if power_o is None else power_o + o2
    lead, rest = parts(amp[0])
    a = dot(cols2(order[1], order[1]), rows2(lead, rest))
    lead, rest = parts(a)
    a = dot(cols2(lead, rest), rows2(order[0], order[0]))
    ratio_e = lft(a) * lax.rsqrt(power_e + 1.0)
    ratio_o = rgt(a) * lax.rsqrt(power_o + 1.0)
    ratio_e, ratio_o = cols2(ratio_e, ratio_e), cols2(ratio_o, ratio_o)
    obj_re = obj_im = None
    for m in range(MODES):
        qr, qi = probe[m, 0], probe[m, 1]
        nr, ni = inverse(tab, far[m, 0] * ratio_e, far[m, 1] * ratio_o)
        dr = dual[0, m, 0] + (qr * pr - qi * pi) - nr
        di = dual[0, m, 1] + (qr * pi + qi * pr) - ni
        dual_new[0, m, 0] = dr
        dual_new[0, m, 1] = di
        tr, ti = nr - dr, ni - di
        sums[2 * m] += pr * tr + pi * ti
        sums[2 * m + 1] += pr * ti - pi * tr
        re = qr * tr + qi * ti
        im = qr * ti - qi * tr
        obj_re = re if obj_re is None else obj_re + re
        obj_im = im if obj_im is None else obj_im + im
    for a in range(2):
        for b in range(2):
            for p, value in enumerate((obj_re, obj_im)):
                parts_out[0, a, b, p] = value[a * H:(a + 1) * H, b * H:(b + 1) * H]
    line = lax.broadcasted_iota(jnp.int32, (8, H), 0)
    lane = lax.broadcasted_iota(jnp.int32, (8, H), 1)
    count[...] += jnp.where((line == place[f, 0] // H) & (lane == place[f, 1] // H), 1.0, 0.0)

    @pl.when(f == pl.num_programs(0) - 1)
    def _():
        for c in pending:
            c.wait()


def frames(place, amp, patches, dual, probe, obj):
    n = amp.shape[0]
    tab, order = jnp.asarray(dft_tables()), jnp.asarray(order_table())
    whole = lambda *d: pl.BlockSpec(d, lambda f: (0,) * len(d))
    any_ = pl.BlockSpec(memory_space=pl.ANY)
    ext = pl.BlockSpec(memory_space=pl.ANY)
    f32 = lambda *d: jax.ShapeDtypeStruct(d, F32)
    v = lambda *d: pltpu.VMEM(d, F32)
    return pl.pallas_call(
        frame_kernel,
        grid=(n,),
        in_specs=[
            pl.BlockSpec(memory_space=pltpu.SMEM),
            pl.BlockSpec((1, N, N), lambda f: (f, 0, 0)),
            pl.BlockSpec((1, 2, N, N), lambda f: (f, 0, 0, 0)),
            pl.BlockSpec((1, MODES, 2, N, N), lambda f: (f, 0, 0, 0, 0)),
            whole(MODES, 2, N, N),
            whole(4, 2, N, N),
            whole(2, N, N),
            any_,
        ],
        out_specs=[
            pl.BlockSpec((1, MODES, 2, N, N), lambda f: (f, 0, 0, 0, 0)),
            pl.BlockSpec((1, 2, 2, 2, H, H), lambda f: (f, 0, 0, 0, 0, 0)),
            whole(7, N, N),
            whole(8, H),
            ext, ext, ext, ext,
        ],
        out_shape=[
            f32(*dual.shape), f32(n, 2, 2, 2, H, H), f32(7, N, N), f32(8, H),
            f32(2, 2, TILE, H), f32(2, TILES, BAND, H), f32(2, TILE, H), f32(2, TILES, 8, H),
        ],
        scratch_shapes=[
            v(MODES, 2, N, N), v(2, 2, BAND + 8, H), v(2, BAND + 8, H), v(2, TILES, BAND, H), v(2, TILES, 8, H),
            pltpu.SemaphoreType.DMA((12,)), pltpu.SemaphoreType.DMA((13,)), pltpu.SemaphoreType.DMA((13,)),
        ],
        compiler_params=pltpu.CompilerParams(
            collective_id=2, has_side_effects=True, vmem_limit_bytes=56 << 20),
    )(place, amp, patches, dual, probe, tab, order, obj)


SPAN, FIRST = 656, 120
EDGE = 280
SIDE = 56


def object_kernel(canvas_in, sums, probe, count, obj, east, below, west, above, field, probe_new,
                  canvas, cl, cr, pk_l, pk_r, in_l, in_r, bd, bu, bdh, buh, side_t, side_b, hrow_t, hrow_b,
                  f0, f1, fin, wgt, e0, e1, er, ew, wst, abv, cnt, pwr, window,
                  pair_in, half, in_1, quarter, in_2, chunk, z_all, cnt_l, cnt_r, cnt_a, cnt_u, cnt_d,
                  load_sem, send_sem, recv_sem):
    i, j = lax.axis_index("row"), lax.axis_index("col")
    y, z, x, core = i // 4, i % 4, j // 2, j % 2
    up, down = ((i + 15) % 16, j), ((i + 1) % 16, j)
    lf, rt = (i, (j + 7) % 8), (i, (j + 1) % 8)
    twin = (i, x * 2 + 1 - core)
    ys = [(((y + d) % 4) * 4 + z, j) for d in (1, 2, 3)]
    xs = [(i, ((x + d) % 4) * 2 + core) for d in (1, 2, 3)]
    zs = [(y * 4 + (z + d) % 4, j) for d in (1, 2, 3)]
    peers = [up, down, lf, rt, twin] + ys + xs + zs

    barrier = pltpu.get_barrier_semaphore()
    for p in peers:
        pl.semaphore_signal(barrier, inc=1, device_id=p, device_id_type=MESH)
    load = pltpu.make_async_copy(canvas_in, canvas.at[:, pl.ds(0, 7)], load_sem.at[0])
    load.start()
    loads = [
        pltpu.make_async_copy(below, e0.at[:, :, pl.ds(8, BAND)], load_sem.at[1]),
        pltpu.make_async_copy(below.at[:, :, pl.ds(0, 8)], f0.at[:, :, pl.ds(SPAN - 8, 8)], load_sem.at[2]),
        pltpu.make_async_copy(west, wst, load_sem.at[3]),
        pltpu.make_async_copy(above, abv, load_sem.at[4]),
    ]
    for rows, to, at in ((pl.ds(FIRST, SPAN - 8), f0, pl.ds(0, SPAN - 8)), (pl.ds(LOW, 8), e0, pl.ds(0, 8)),
                         (pl.ds(0, BAND), e0, pl.ds(ROWS - LOW, BAND))):
        for t in range(6):
            loads.append(pltpu.make_async_copy(
                obj.at[:, rows, pl.ds(H * t, H)], to.at[:, t, at], load_sem.at[1 + len(loads)]))
        loads.append(pltpu.make_async_copy(east.at[:, :, rows], to.at[:, pl.ds(6, 2), at], load_sem.at[1 + len(loads)]))
    for c in loads:
        c.start()

    used = [0]
    started = []

    def send(src, dst, to):
        k = used[0]
        used[0] += 1
        c = pltpu.make_async_remote_copy(
            src_ref=src, dst_ref=dst, send_sem=send_sem.at[k], recv_sem=recv_sem.at[k],
            device_id=to, device_id_type=MESH,
        )
        c.start()
        started.append(c)
        return c

    def landed(*copies):
        for c in copies:
            c.wait_recv()

    other = pl.ds(pl.multiple_of((1 - core) * H, H), H)
    mine = pl.ds(pl.multiple_of(core * H, H), H)

    load.wait()

    lane3 = lax.broadcasted_iota(jnp.int32, (2, SIDE, H), 2)
    pk_l[...] = jnp.zeros_like(pk_l)
    pk_r[...] = jnp.zeros_like(pk_r)

    def pack(q, carry):
        at = pl.ds(pl.multiple_of(q * SIDE, 8), SIDE)
        pk_l[...] += pltpu.roll(jnp.where(lane3 < 4, canvas[:, 1, at], 0.0), q * 8, 2)
        pk_r[...] += pltpu.roll(jnp.where(lane3 >= H - 4, canvas[:, 5, at], 0.0), q * 8, 2)
        return carry

    lax.fori_loop(0, 16, pack, 0)
    pl.semaphore_wait(barrier, len(peers))

    top_rows, low_rows, mid = pl.ds(0, BAND), pl.ds(LOW, BAND), pl.ds(BAND, LOW - BAND)
    ends = [
        send(pk_r, in_l, rt), send(pk_l, in_r, lf),
        send(count, cnt_l, rt), send(count, cnt_r, lf),
    ]
    for rows in (top_rows, low_rows):
        ends.append(send(canvas.at[:, 6, rows], cl.at[:, rows], rt))
        ends.append(send(canvas.at[:, 0, rows], cr.at[:, rows], lf))
    a_pair = send(sums.at[:, other], pair_in, twin)
    inner = pl.ds(1, 5)
    bands = [
        send(canvas.at[:, inner, pl.ds(0, H)], bd.at[:, inner], up),
        send(canvas.at[:, inner, pl.ds(TILE, H)], bu.at[:, inner], down),
    ]
    rest = [
        send(canvas.at[:, 6, mid], cl.at[:, mid], rt),
        send(canvas.at[:, 0, mid], cr.at[:, mid], lf),
    ]

    power = None
    for m in range(2 * MODES):
        q = probe[m] * probe[m]
        power = q if power is None else power + q
    for a in range(2):
        for b in range(2):
            pwr[a, b] = power[a * H:(a + 1) * H, b * H:(b + 1) * H].reshape(16, 8, H)

    landed(*ends)
    for c in ends:
        c.wait_send()
    keep = (lane3 < 4) | (lane3 >= H - 4)

    def unpack(q, carry):
        at = pl.ds(pl.multiple_of(q * SIDE, 8), SIDE)
        both = in_l[...] + in_r[...]
        canvas[:, 7, at] = jnp.where(keep, pltpu.roll(both, (H - q * 8) % H, 2), 0.0)
        return carry

    lax.fori_loop(0, 16, unpack, 0)

    def widen(first, side):
        def step(g, carry):
            at, src = pl.ds(pl.multiple_of(g * 8, 8), 8), pl.ds(pl.multiple_of(first + g * 8, 8), 8)
            side[:, 0, at] = canvas[:, 0, src] + cl[:, src]
            side[:, 1, at] = canvas[:, 6, src] + cr[:, src]
            side[:, 2, at] = canvas[:, 7, src]
            return carry

        lax.fori_loop(0, 16, step, 0)

    widen(0, side_t)
    widen(TILE, side_b)
    for row, hrow in ((H, hrow_t), (LOW, hrow_b)):
        at = pl.ds(row, 8)
        hrow[...] = canvas[:, :, at]
        hrow[:, 0] += cl[:, at]
        hrow[:, 6] += cr[:, at]
    lane2 = lax.broadcasted_iota(jnp.int32, (8, H), 1)
    cnt_a[...] = jnp.where(
        lane2 < 2, pltpu.roll(cnt_l[...], H - 4, 1),
        jnp.where(lane2 < 8, pltpu.roll(count[...], 2, 1), jnp.where(lane2 < 10, pltpu.roll(cnt_r[...], 8, 1), 0.0)),
    )
    counts = [send(cnt_a, cnt_d, up), send(cnt_a, cnt_u, down)]
    one, two = pl.ds(0, 1), pl.ds(6, 2)
    bands += [
        send(hrow_t, bdh, up), send(hrow_b, buh, down),
        send(side_t.at[:, one], bd.at[:, one], up), send(side_b.at[:, one], bu.at[:, one], down),
        send(side_t.at[:, pl.ds(1, 2)], bd.at[:, two], up), send(side_b.at[:, pl.ds(1, 2)], bu.at[:, two], down),
    ]

    landed(a_pair)
    half[...] = sums[:, mine] + pair_in[...]
    lanes = (pl.ds(0, H), pl.ds(H, H))
    path = (((y, ys), (x, xs)), ((x, xs), (y, ys)))

    def eights(at, n):
        return pl.ds(pl.multiple_of(at, 8), n)

    stage_1 = []
    for q in range(2):
        here, to = path[q][0]
        for d in (1, 2, 3):
            stage_1.append(send(half.at[:, eights(((here + d) % 4) * 32, 32), lanes[q]], in_1.at[q, d - 1], to[d - 1]))

    landed(*counts)
    line = lax.broadcasted_iota(jnp.int32, (8, H), 0)
    window[pl.ds(0, 8)] = jnp.where(line < 2, pltpu.roll(cnt_u[...], 4, 0), pltpu.roll(cnt_a[...], 2, 0))
    window[pl.ds(8, 8)] = jnp.where(line < 2, cnt_d[...], 0.0)
    wide_lane = lax.broadcasted_iota(jnp.int32, (H, TILES * H), 1)
    slot = lax.broadcasted_iota(jnp.int32, (H, TILES * H), 0)
    block_of = jnp.where(wide_lane >= 7 * H + H // 2, -1, wide_lane // H)
    for b in range(2):
        pick = jnp.where(slot == block_of - b + 2, 1.0, 0.0).astype(BF16)
        wide = dot(window[...].astype(BF16), pick)
        for r in range(10):
            row = jnp.broadcast_to(wide[r:r + 1], (8, TILES * H))
            for t in range(TILES):
                cnt[b, r, t] = row[:, t * H:(t + 1) * H]

    tile = lax.broadcasted_iota(jnp.int32, (TILES, 8, H), 0)
    sub = lax.broadcasted_iota(jnp.int32, (TILES, 8, H), 1)
    lane = lax.broadcasted_iota(jnp.int32, (TILES, 8, H), 2)
    col = jnp.where(tile < 7, tile * H + lane, jnp.where(lane < H // 2, 7 * H + lane, lane - H)) + j * TILE
    col_ok = (col >= 0) & (col < 8 * TILE) & ((tile < 7) | (lane < 4) | (lane >= H - 4))
    lane1 = lax.broadcasted_iota(jnp.int32, (8, H), 1)

    def density(r, g):
        den = None
        for a in range(2):
            for b in range(2):
                term = cnt[b, r - a + 2] * pwr[a, b, g][None]
                den = term if den is None else den + term
        return den

    def finish(src, at, to, w, ok, den, total):
        inv = jnp.where(ok, 1.0 / (den + (0.5 + 4.0 * 16.0)), 0.0)
        w[:, at] = 16.0 * inv
        for p in range(2):
            value = jnp.where(ok, src[p, :, at], 0.0)
            src[p, :, at] = value
            to[p] = (total[p] + 0.5 * value) * inv

    for c in loads:
        c.wait()
    for c in rest:
        c.wait()

    def whole_rows(p, rows):
        return jnp.concatenate(
            [canvas[p, pl.ds(0, 1), rows] + cl[p, rows][None], canvas[p, pl.ds(1, 5), rows],
             canvas[p, pl.ds(6, 1), rows] + cr[p, rows][None], canvas[p, pl.ds(7, 1), rows]], axis=0)

    def outer_tile(src, at, rows):
        for p in range(2):
            src[p, 7, at] = jnp.where(lane1 < 4, src[p, 7, at], wst[p, rows])

    for e, row in ((0, LOW), (EDGE - 8, H)):
        at = pl.ds(e, 8)
        for p in range(2):
            er[p, :, at] = whole_rows(p, pl.ds(row, 8))

    def prepare(n, carry):
        r, g = 1 + n // 16, n % 16
        row = H + n * 8
        rows, at = eights(row, 8), eights(row - FIRST, 8)
        outer_tile(f0, at, rows)
        total = [whole_rows(p, rows) for p in range(2)]

        class To:
            def __setitem__(self, p, value):
                canvas[p, :, rows] = value

        finish(f0, at, To(), wgt, col_ok, density(r, g), total)
        return carry

    lax.fori_loop(0, 80, prepare, 0)
    for at, rows in ((pl.ds(0, 8), pl.ds(H - 8, 8)), (pl.ds(SPAN - 8, 8), None)):
        wgt[:, at] = jnp.zeros((TILES, 8, H), F32)
        row_ok = (i < 15) if rows is None else (i >= 0)
        if rows is not None:
            outer_tile(f0, at, rows)
        for p in range(2):
            f0[p, :, at] = jnp.where(col_ok & row_ok, f0[p, :, at], 0.0)

    def sweep(src, a, dst, b, rhs, c, w, stride, unroll):
        rows = lambda o, t: (slice(None), slice(None), pl.ds(o + t, 8, stride=stride), slice(None))
        lane4 = lane[None]

        def update(t, over, here, under):
            left_ = jnp.concatenate([here[:, 7:], here[:, :7]], axis=1)
            right_ = jnp.concatenate([here[:, 1:], here[:, :1]], axis=1)
            left_ = pltpu.roll(jnp.where(lane4 == H - 1, left_, here), 1, 3)
            right_ = pltpu.roll(jnp.where(lane4 == 0, right_, here), H - 1, 3)
            near = (over + under) + (left_ + right_)
            dst[rows(b, t)] = rhs[rows(c, t)] + w[:, pl.ds(t, 8, stride=stride), :][None] * near

        first, last = src[rows(a, 0)], src[rows(a, stride - 1)]

        def step(t, carry):
            over, here = carry
            under = src[rows(a, t + 1)]
            update(t, over, here, under)
            return here, under

        over, here = lax.fori_loop(0, stride - 1, step, (pltpu.roll(last, 1, 2), first), unroll=unroll)
        update(stride - 1, over, here, pltpu.roll(first, 7, 2))

    landed(*stage_1)
    for q in range(2):
        here, _ = path[q][0]
        quarter[q] = half[:, eights(here * 32, 32), lanes[q]] + in_1[q, 0] + in_1[q, 1] + in_1[q, 2]
    stage_2 = []
    for q in range(2):
        here, to = path[q][1]
        for d in (1, 2, 3):
            stage_2.append(send(quarter.at[q, :, eights(((here + d) % 4) * 8, 8)], in_2.at[q, d - 1], to[d - 1]))
    sweep(f0, 0, f1, 0, canvas, FIRST, wgt, SPAN // 8, 9)
    landed(*stage_2)
    for q in range(2):
        here, _ = path[q][1]
        chunk[q] = quarter[q, :, eights(here * 8, 8)] + in_2[q, 0] + in_2[q, 1] + in_2[q, 2]
    z_all[pl.ds(z, 1)] = chunk[...][None]
    stage_3 = [send(chunk, z_all.at[z], to) for to in zs]
    sweep(f1, 0, f0, 0, canvas, FIRST, wgt, SPAN // 8, 9)
    landed(*stage_3)
    stage_4 = []
    for q in range(2):
        (outer, _), (in_, to) = path[q]
        total = z_all[0, q] + z_all[1, q] + z_all[2, q] + z_all[3, q]
        at = eights(core * H + outer * 32 + in_ * 8, 8)
        probe_new[:, at, lanes[q]] = (total[:6] + probe[:, at, lanes[q]]) / (total[6:] + 1.0)
        here = probe_new.at[:, at, lanes[q]]
        stage_4 += [send(here, here, p) for p in to]
    sweep(f0, 0, f1, 0, canvas, FIRST, wgt, SPAN // 8, 9)
    landed(*stage_4)
    stage_5 = []
    for q in range(2):
        outer, to = path[q][0]
        here = probe_new.at[:, eights(core * H + outer * 32, 32), lanes[q]]
        stage_5 += [send(here, here, p) for p in to]
    sweep(f1, 0, fin, FIRST, canvas, FIRST, wgt, SPAN // 8, 9)

    outs = []

    def copy_out(rows):
        c = pltpu.make_async_copy(fin.at[:, pl.ds(0, 7), rows], field.at[:, :, rows], load_sem.at[26 + len(outs)])
        c.start()
        outs.append(c)

    copy_out(mid)

    landed(*bands)

    def edge_step(e, r, g, rows, total, ok):
        at = pl.ds(e, 8) if isinstance(e, int) else eights(e, 8)
        if rows is not None:
            outer_tile(e0, at, rows)

        class To:
            def __setitem__(self, p, value):
                er[p, :, at] = value

        finish(e0, at, To(), ew, col_ok & ok, density(r, g), total)

    for e, row, r, g in ((0, LOW, 5, 15), (EDGE - 8, H, 1, 0)):
        edge_step(e, r, g, pl.ds(row, 8), [er[p, :, pl.ds(e, 8)] for p in range(2)], i >= 0)

    def lower(g, carry):
        rows = eights(TILE + g * 8, 8)
        at = eights(g * 8, 8)
        total = [bd[p, :, at] + whole_rows(p, rows) for p in range(2)]
        edge_step(8 + g * 8, 6, g, None, total, i < 15)
        return carry

    def upper(g, carry):
        rows = eights(g * 8, 8)
        total = [bu[p, :, rows] + whole_rows(p, rows) for p in range(2)]
        edge_step(ROWS - LOW + g * 8, 0, g, rows, total, i >= 0)
        return carry

    lax.fori_loop(0, 16, lower, 0)
    lax.fori_loop(0, 16, upper, 0)
    at = pl.ds(H + 8, 8)
    for p in range(2):
        e0[p, :, at] = jnp.where(sub < 4, e0[p, :, at], abv[p])
    total = [jnp.where(sub < 4, bdh[p], buh[p]) for p in range(2)]
    den = None
    for a in range(2):
        for b in range(2):
            low = cnt[b, 7 - a + 2] * pwr[a, b, 0][None]
            high = cnt[b, -1 - a + 2] * pwr[a, b, 15][None]
            term = jnp.where(sub < 4, low, high)
            den = term if den is None else den + term
    row_ok = ((sub < 4) & (i < 15)) | ((sub >= 4) & (i > 0))

    class To:
        def __setitem__(self, p, value):
            er[p, :, at] = value

    finish(e0, at, To(), ew, col_ok & row_ok, den, total)

    landed(*stage_5)
    here = probe_new.at[:, mine]
    stage_6 = send(here, here, twin)
    sweep(e0, 0, e1, 0, er, 0, ew, EDGE // 8, 17)
    sweep(e1, 0, e0, 0, er, 0, ew, EDGE // 8, 17)
    sweep(e0, 0, e1, 0, er, 0, ew, EDGE // 8, 17)
    sweep(e1, 0, e0, 0, er, 0, ew, EDGE // 8, 17)

    def place_edges(g, carry):
        at = eights(g * 8, 8)
        fin[:, :, at] = e0[:, :, eights(ROWS - LOW + g * 8, 8)]
        fin[:, :, eights(TILE + g * 8, 8)] = e0[:, :, eights(8 + g * 8, 8)]
        return carry

    lax.fori_loop(0, 16, place_edges, 0)
    sub4 = sub[None]
    at = pl.ds(H, 8)
    fin[:, :, at] = jnp.where(sub4 < 4, e0[:, :, pl.ds(EDGE - 8, 8)], fin[:, :, at])
    at = pl.ds(LOW, 8)
    fin[:, :, at] = jnp.where(sub4 < 4, fin[:, :, at], e0[:, :, pl.ds(0, 8)])
    copy_out(pl.ds(0, BAND))
    copy_out(pl.ds(LOW, BAND))
    landed(stage_6)
    for c in outs:
        c.wait()
    for c in started:
        if not any(c is k for k in ends + rest):
            c.wait_send()


def update_object(canvas, sums, probe, count, obj, east, below, west, above):
    f32 = lambda *d: jax.ShapeDtypeStruct(d, F32)
    vm, any_ = pl.BlockSpec(memory_space=pltpu.VMEM), pl.BlockSpec(memory_space=pl.ANY)
    v = lambda *d: pltpu.VMEM(d, F32)
    small = v(8, H)
    return pl.pallas_call(
        object_kernel,
        out_shape=[f32(2, 7, WIDE, H), f32(6, N, N)],
        in_specs=[any_, vm, vm, vm, any_, any_, any_, any_, any_],
        out_specs=[any_, vm],
        scratch_shapes=[
            v(2, TILES, WIDE, H), v(2, WIDE, H), v(2, WIDE, H),
            v(2, SIDE, H), v(2, SIDE, H), v(2, SIDE, H), v(2, SIDE, H),
            v(2, TILES, H, H), v(2, TILES, H, H), v(2, TILES, 8, H), v(2, TILES, 8, H),
            v(2, 3, H, H), v(2, 3, H, H), v(2, TILES, 8, H), v(2, TILES, 8, H),
            v(2, TILES, SPAN, H), v(2, TILES, SPAN, H), v(2, TILES, WIDE, H), v(TILES, SPAN, H),
            v(2, TILES, EDGE, H), v(2, TILES, EDGE, H), v(2, TILES, EDGE, H), v(TILES, EDGE, H),
            v(2, TILE, H), v(2, TILES, 8, H), v(2, 10, TILES, 8, H), v(2, 2, 16, 8, H), v(16, H),
            v(7, H, N), v(7, H, N), v(2, 3, 7, 32, H), v(2, 7, 32, H), v(2, 3, 7, 8, H), v(2, 7, 8, H),
            v(4, 2, 7, 8, H), small, small, small, small, small,
            pltpu.SemaphoreType.DMA((30,)), pltpu.SemaphoreType.DMA((56,)), pltpu.SemaphoreType.DMA((56,)),
        ],
        compiler_params=pltpu.CompilerParams(
            collective_id=1, has_side_effects=True, vmem_limit_bytes=62 << 20
        ),
    )(canvas, sums, probe, count, obj, east, below, west, above)


def place_kernel(place, parts_in, canvas):
    canvas[...] = jnp.zeros_like(canvas)
    for f in range(parts_in.shape[0]):
        r, c = pl.multiple_of(place[f, 0], H), place[f, 1] // H
        for a in range(2):
            for b in range(2):
                for p in range(2):
                    canvas[p, c + b, pl.ds(r + a * H, H)] += parts_in[f, a, b, p]


def place_frames(place, con):
    vm = pl.BlockSpec(memory_space=pltpu.VMEM)
    return pl.pallas_call(
        place_kernel,
        out_shape=jax.ShapeDtypeStruct((2, 7, WIDE, H), F32),
        in_specs=[pl.BlockSpec(memory_space=pltpu.SMEM), vm],
        out_specs=vm,
        compiler_params=pltpu.CompilerParams(vmem_limit_bytes=40 << 20),
    )(place, con)


def window_kernel(place, field, object_new, patches_new, sems):
    outs = []
    for t in range(6):
        outs.append(pltpu.make_async_copy(
            field.at[:, t, pl.ds(0, TILE)], object_new.at[:, :, pl.ds(H * t, H)], sems.at[t]))
    for f in range(place.shape[0]):
        r, c = pl.multiple_of(place[f, 0], H), place[f, 1] // H
        for t in range(2):
            outs.append(pltpu.make_async_copy(
                field.at[:, c + t, pl.ds(r, N)], patches_new.at[f, :, :, pl.ds(H * t, H)], sems.at[6 + 2 * f + t]))
    for c in outs:
        c.start()
    for c in outs:
        c.wait()


def windows(place, field):
    vm, any_ = pl.BlockSpec(memory_space=pltpu.VMEM), pl.BlockSpec(memory_space=pl.ANY)
    f32 = lambda *d: jax.ShapeDtypeStruct(d, F32)
    n = place.shape[0]
    return pl.pallas_call(
        window_kernel,
        out_shape=[f32(2, TILE, TILE), f32(n, 2, N, N)],
        in_specs=[pl.BlockSpec(memory_space=pltpu.SMEM), vm],
        out_specs=[any_, any_],
        scratch_shapes=[pltpu.SemaphoreType.DMA((6 + 2 * n,))],
        compiler_params=pltpu.CompilerParams(vmem_limit_bytes=40 << 20),
    )(place, field)


def per_device(amplitude, patches, dual, probe, obj, positions):
    spot = jnp.stack([lax.axis_index("row"), lax.axis_index("col")]).astype(jnp.int32)
    place = positions - spot * TILE
    dual_new, con, sums, count, *around = frames(place, amplitude, patches, dual, probe, obj)
    canvas = place_frames(place, con)
    field, probe_new = update_object(canvas, sums, probe.reshape(2 * MODES, N, N), count, obj, *around)
    object_new, patches_new = windows(place, field)
    return dual_new, object_new, probe_new.reshape(probe.shape), patches_new


def solution(mesh):
    return jax.shard_map(
        per_device,
        mesh=mesh,
        in_specs=(
            P(("row", "col"), None, None),
            P(("row", "col"), None, None, None),
            P(("row", "col"), None, None, None, None),
            P(),
            P(None, "row", "col"),
            P(("row", "col"), None),
        ),
        out_specs=(
            P(("row", "col"), None, None, None, None),
            P(None, "row", "col"),
            P(),
            P(("row", "col"), None, None, None),
        ),
        check_vma=False,
    )
```

time: 384 us -> 124 us (0.32)
  waiting for transfers between devices: 133 us -> 0 us
  Pallas kernels: 28.9 us -> 109 us
  starting transfers between devices: 78.5 us -> 0 us
  other arithmetic: 70.4 us -> 0.66 us
  local copies, waits for them, and re-layouts: 55.9 us -> 12.8 us
  between operations: 14.5 us -> 0.7 us
    psum x1 -> x0, waiting for transfers between devices: 98 us -> none  [per_device(): totals = lax.psum(packed, ('row', 'col'))]
    pallas_call x1 -> x4, Pallas kernels: 28.9 us -> 109 us  [the longest x1 68.7 us: update_object(): pl.pallas_call(object_kernel, out_shape=[f32(2, 7, WIDE, H), f32(6, N, N)...]
    ppermute x20 -> x0, starting transfers between devices: 78.5 us -> none  [the longest x8 59.8 us: extended_2(): lax.ppermute(lax.slice_in_dim(block, block.shape[dim] - width, None, axis...]
    div x6 -> x0, other arithmetic: 50.6 us -> none  [the longest x5 50.2 us: per_device(): field = (rhs + smooth_weight * neighbours(padded)) / diagonal]
    ppermute x20 -> x0, waiting for transfers between devices: 35.2 us -> none  [the longest x4 23.3 us: from_behind(): return lax.ppermute(block, axis, route)]
    slice x16 -> x0, local copies, waits for them, and re-layouts: 19.7 us -> none  [the longest x8 5.45 us: extended_2(): lax.slice_in_dim(block, block.shape[dim] - width, None, axis=dim)]
    gather x12 -> x0, local copies, waits for them, and re-layouts: 16.4 us -> none
    ppermute x8 -> x0, local copies, waits for them, and re-layouts: 9.64 us -> none  [the longest x4 4.89 us: extended_2(): lax.ppermute(lax.slice_in_dim(block, 0, width, axis=dim), axis, backward)]
  transfers between devices with their start and end apart: 21 -> 0, of which waited for: 7 -> 0; matrix products, arithmetic and copies ran while one was open for 17% -> 0% of each run, Pallas kernels for 0% -> 0%
where the time goes in v2:
time: 124 us; the launch traced here: 123 us
  Pallas kernels  109 us (88%)
  local copies, waits for them, and re-layouts  12.8 us (10%)
    pallas_call x1, Pallas kernels, update_object(): pl.pallas_call(object_kernel, out_shape=[f32(2, 7, WIDE, H), f32(6, N, N)...  68.7 us
    pallas_call x1, Pallas kernels, frames(): pl.pallas_call(frame_kernel, grid=(n,), in_specs=[pl.BlockSpec(memory_spa...  35.3 us
    unnamed x15, local copies, waits for them, and re-layouts  12.8 us
    pallas_call x1, Pallas kernels, windows(): pl.pallas_call(window_kernel, out_shape=[f32(2, TILE, TILE), f32(n, 2, N,...  4.09 us

profile of v2, /device:TPU:0, one launch (start us, length us, event | category | flops | bytes accessed | tf_op | source)
XLA Modules:
  0.0 123.5 jit_solution(15937330474773733181)
XLA Ops:
  0.6 0.1 add_multiply_fusion
  0.7 0.8 copy.12
  1.5 0.6 broadcast_subtract_fusion.place
  2.1 0.0 copy-start.3
  2.1 35.3 %shard_map.111 = (f32[4,3,2,256,256]{4,3,2,1,0:T(8,128)}, f32[4,2,2,2,128,128]{5,4,3,2,1,0:T(8,128)}, f32[7,256,256]{2,1,0:T(8,128)}, f32[8,128]{1,0:T(8,128)}, ...) custom-call(s32[4,2]{1,0:T(4,128)} %broadcast_subtract_fusion.place,, ...), custom_call_target="tpu_custom_call" | custom-call | tf_op jit(solution)/shard_map/pallas_call | solution.py:256
  37.4 0.0 copy-done.3
  37.4 0.0 copy-start.2
  37.4 1.6 %copy-done.2 = f32[4,2,2,2,128,128]{5,4,3,2,1,0:T(8,128)S(1)} copy-done((f32[4,2,2,2,128,128]{5,4,3,2,1,0:T(8,128)S(1)}, f32[4,2,2,2,128,128]{5,4,3,2,1,0:T(8,128)}, u32[]{:S(2)}) %copy-start.2) | copy-done | bytes 2097176
  39.0 1.2 shard_map.112.canvas_in
  40.2 0.0 copy-start
  40.2 2.7 %copy-done = f32[2,7,896,128]{3,2,1,0:T(8,128)} copy-done((f32[2,7,896,128]{3,2,1,0:T(8,128)}, f32[2,7,896,128]{3,2,1,0:T(8,128)S(1)}, u32[]{:S(2)}) %copy-start) | copy-done | bytes 6422552
  42.9 68.7 %shard_map.113 = (f32[2,7,896,128]{3,2,1,0:T(8,128)}, f32[6,256,256]{2,1,0:T(8,128)}) custom-call(f32[2,7,896,128]{3,2,1,0:T(8,128)} %copy-done, f32[7,256,256]{2,1,0:T(8,128)} %get-tuple-element.18.sums, f32[6,256,256]{2,1,0:T(8,128)} %bitcast.4, f32[8,128]{1,0:T(8,128)} %get-tuple-element.19.count, f32[2,768,768]{2,1,0:T(8,128)} %obj.3, ...), custom_call_target="tpu_custom_call" | custom-call | tf_op jit(solution)/shard_map/pallas_call | solution.py:681
  111.6 0.0 copy-start.1
  111.6 2.8 %copy-done.1 = f32[2,7,896,128]{3,2,1,0:T(8,128)S(1)} copy-done((f32[2,7,896,128]{3,2,1,0:T(8,128)S(1)}, f32[2,7,896,128]{3,2,1,0:T(8,128)}, u32[]{:S(2)}) %copy-start.1) | copy-done | bytes 6422552
  114.5 0.0 copy-start.4
  114.5 4.1 %shard_map.114 = (f32[2,768,768]{2,1,0:T(8,128)}, f32[4,2,256,256]{3,2,1,0:T(8,128)}) custom-call(s32[4,2]{1,0:T(4,128)S(1)} %copy-done.3, f32[2,7,896,128]{3,2,1,0:T(8,128)S(1)} %copy-done.1), custom_call_target="tpu_custom_call" | custom-call | tf_op jit(solution)/shard_map/pallas_call | solution.py:745
  118.6 1.1 copy-done.4
  119.6 0.0 copy-start.5
  119.6 2.7 %copy.15 = f32[4,3,2,256,256]{4,3,2,1,0:T(8,128)} copy(f32[4,3,2,256,256]{4,3,2,1,0:T(8,128)S(1)} %copy-done.4) | data formatting | bytes 12582912
  122.3 0.0 copy-done.5
  122.4 1.1 copy.16
Async XLA Ops:
  2.1 35.3 %copy-start.3 = (s32[4,2]{1,0:T(4,128)S(1)}, s32[4,2]{1,0:T(4,128)}, u32[]{:S(2)}) copy-start(s32[4,2]{1,0:T(4,128)} %broadcast_subtract_fusion.place) | copy-start | bytes 100
  37.4 1.6 %copy-start.2 = (f32[4,2,2,2,128,128]{5,4,3,2,1,0:T(8,128)S(1)}, f32[4,2,2,2,128,128]{5,4,3,2,1,0:T(8,128)}, u32[]{:S(2)}) copy-start(f32[4,2,2,2,128,128]{5,4,3,2,1,0:T(8,128)} %get-tuple-element.17.parts_in) | copy-start | bytes 6291460
  40.2 2.7 %copy-start = (f32[2,7,896,128]{3,2,1,0:T(8,128)}, f32[2,7,896,128]{3,2,1,0:T(8,128)S(1)}, u32[]{:S(2)}) copy-start(f32[2,7,896,128]{3,2,1,0:T(8,128)S(1)} %shard_map.112.canvas_in) | copy-start | bytes 19267588
  111.6 2.8 %copy-start.1 = (f32[2,7,896,128]{3,2,1,0:T(8,128)S(1)}, f32[2,7,896,128]{3,2,1,0:T(8,128)}, u32[]{:S(2)}) copy-start(f32[2,7,896,128]{3,2,1,0:T(8,128)} %get-tuple-element.24.field) | copy-start | bytes 19267588
  114.5 5.2 %copy-start.4 = (f32[4,3,2,256,256]{4,3,2,1,0:T(8,128)S(1)}, f32[4,3,2,256,256]{4,3,2,1,0:T(8,128)}, u32[]{:S(2)}) copy-start(f32[4,3,2,256,256]{4,3,2,1,0:T(8,128)} %get-tuple-element.32) | copy-start | bytes 18874372
  119.6 2.7 %copy-start.5 = (f32[6,256,256]{2,1,0:T(8,128)S(1)}, f32[6,256,256]{2,1,0:T(8,128)}, u32[]{:S(2)}) copy-start(f32[6,256,256]{2,1,0:T(8,128)} %get-tuple-element.26) | copy-start | bytes 4718596

commit v3 on v2

--- a/solution.py
+++ b/solution.py
@@ -363,6 +363,7 @@
     pl.semaphore_wait(barrier, len(peers))
 
     top_rows, low_rows, mid = pl.ds(0, BAND), pl.ds(LOW, BAND), pl.ds(BAND, LOW - BAND)
+    a_pair = send(sums.at[:, other], pair_in, twin)
     ends = [
         send(pk_r, in_l, rt), send(pk_l, in_r, lf),
         send(count, cnt_l, rt), send(count, cnt_r, lf),
@@ -370,7 +371,6 @@
     for rows in (top_rows, low_rows):
         ends.append(send(canvas.at[:, 6, rows], cl.at[:, rows], rt))
         ends.append(send(canvas.at[:, 0, rows], cr.at[:, rows], lf))
-    a_pair = send(sums.at[:, other], pair_in, twin)
     inner = pl.ds(1, 5)
     bands = [
         send(canvas.at[:, inner, pl.ds(0, H)], bd.at[:, inner], up),
@@ -388,6 +388,20 @@
     for a in range(2):
         for b in range(2):
             pwr[a, b] = power[a * H:(a + 1) * H, b * H:(b + 1) * H].reshape(16, 8, H)
+
+    landed(a_pair)
+    half[...] = sums[:, mine] + pair_in[...]
+    lanes = (pl.ds(0, H), pl.ds(H, H))
+    path = (((y, ys), (x, xs)), ((x, xs), (y, ys)))
+
+    def eights(at, n):
+        return pl.ds(pl.multiple_of(at, 8), n)
+
+    stage_1 = []
+    for q in range(2):
+        here, to = path[q][0]
+        for d in (1, 2, 3):
+            stage_1.append(send(half.at[:, eights(((here + d) % 4) * 32, 32), lanes[q]], in_1.at[q, d - 1], to[d - 1]))
 
     landed(*ends)
     for c in ends:
@@ -431,20 +445,6 @@
         send(side_t.at[:, one], bd.at[:, one], up), send(side_b.at[:, one], bu.at[:, one], down),
         send(side_t.at[:, pl.ds(1, 2)], bd.at[:, two], up), send(side_b.at[:, pl.ds(1, 2)], bu.at[:, two], down),
     ]
-
-    landed(a_pair)
-    half[...] = sums[:, mine] + pair_in[...]
-    lanes = (pl.ds(0, H), pl.ds(H, H))
-    path = (((y, ys), (x, xs)), ((x, xs), (y, ys)))
-
-    def eights(at, n):
-        return pl.ds(pl.multiple_of(at, 8), n)
-
-    stage_1 = []
-    for q in range(2):
-        here, to = path[q][0]
-        for d in (1, 2, 3):
-            stage_1.append(send(half.at[:, eights(((here + d) % 4) * 32, 32), lanes[q]], in_1.at[q, d - 1], to[d - 1]))
 
     landed(*counts)
     line = lax.broadcasted_iota(jnp.int32, (8, H), 0)
@@ -722,33 +722,39 @@
     )(place, con)
 
 
-def window_kernel(place, field, object_new, patches_new, sems):
+def window_kernel(place, field, object_new, patches_new, held, load_sems, sems):
+    loads = [pltpu.make_async_copy(field.at[:, t], held.at[:, t], load_sems.at[t]) for t in range(7)]
+    for c in loads:
+        c.start()
     outs = []
     for t in range(6):
+        loads[t].wait()
         outs.append(pltpu.make_async_copy(
-            field.at[:, t, pl.ds(0, TILE)], object_new.at[:, :, pl.ds(H * t, H)], sems.at[t]))
+            held.at[:, t, pl.ds(0, TILE)], object_new.at[:, :, pl.ds(H * t, H)], sems.at[t]))
+        outs[-1].start()
+    loads[6].wait()
     for f in range(place.shape[0]):
         r, c = pl.multiple_of(place[f, 0], H), place[f, 1] // H
         for t in range(2):
             outs.append(pltpu.make_async_copy(
-                field.at[:, c + t, pl.ds(r, N)], patches_new.at[f, :, :, pl.ds(H * t, H)], sems.at[6 + 2 * f + t]))
-    for c in outs:
-        c.start()
+                held.at[:, c + t, pl.ds(r, N)], patches_new.at[f, :, :, pl.ds(H * t, H)], sems.at[6 + 2 * f + t]))
+            outs[-1].start()
     for c in outs:
         c.wait()
 
 
 def windows(place, field):
-    vm, any_ = pl.BlockSpec(memory_space=pltpu.VMEM), pl.BlockSpec(memory_space=pl.ANY)
+    any_ = pl.BlockSpec(memory_space=pl.ANY)
     f32 = lambda *d: jax.ShapeDtypeStruct(d, F32)
     n = place.shape[0]
     return pl.pallas_call(
         window_kernel,
         out_shape=[f32(2, TILE, TILE), f32(n, 2, N, N)],
-        in_specs=[pl.BlockSpec(memory_space=pltpu.SMEM), vm],
+        in_specs=[pl.BlockSpec(memory_space=pltpu.SMEM), any_],
         out_specs=[any_, any_],
-        scratch_shapes=[pltpu.SemaphoreType.DMA((6 + 2 * n,))],
-        compiler_params=pltpu.CompilerParams(vmem_limit_bytes=40 << 20),
+        scratch_shapes=[
+            pltpu.VMEM((2, 7, WIDE, H), F32), pltpu.SemaphoreType.DMA((7,)), pltpu.SemaphoreType.DMA((6 + 2 * n,))],
+        compiler_params=pltpu.CompilerParams(vmem_limit_bytes=60 << 20),
     )(place, field)
 
 

time: 124 us -> 122 us (0.984)
    pallas_call x1, Pallas kernels: 68.7 us -> 65.5 us  [update_object(): pl.pallas_call(object_kernel, out_shape=[f32(2, 7, WIDE, H), f32(6, N, N)...]
    pallas_call x1, Pallas kernels: 4.09 us -> 6.43 us  [windows(): pl.pallas_call(window_kernel, out_shape=[f32(2, TILE, TILE), f32(n, 2, N,...]
    unnamed x15 -> x11, local copies, waits for them, and re-layouts: 12.8 us -> 12.4 us
where the time goes in v3:
time: 122 us
  Pallas kernels  108 us (89%)
  local copies, waits for them, and re-layouts  12.4 us (10%)
    pallas_call x1, Pallas kernels, update_object(): pl.pallas_call(object_kernel, out_shape=[f32(2, 7, WIDE, H), f32(6, N, N)...  65.5 us
    pallas_call x1, Pallas kernels, frames(): pl.pallas_call(frame_kernel, grid=(n,), in_specs=[pl.BlockSpec(memory_spa...  35.3 us
    unnamed x11, local copies, waits for them, and re-layouts  12.4 us
    pallas_call x1, Pallas kernels, windows(): pl.pallas_call(window_kernel, out_shape=[f32(2, TILE, TILE), f32(n, 2, N,...  6.43 us

profile of v3, /device:TPU:0, one launch (start us, length us, event | category | flops | bytes accessed | tf_op | source)
XLA Modules:
  0.0 122.2 jit_solution(9304324683702154818)
XLA Ops:
  0.6 0.1 add_multiply_fusion
  0.7 0.8 copy.12
  1.5 0.6 broadcast_subtract_fusion.place
  2.1 0.0 copy-start.2
  2.1 35.3 %shard_map.111 = (f32[4,3,2,256,256]{4,3,2,1,0:T(8,128)}, f32[4,2,2,2,128,128]{5,4,3,2,1,0:T(8,128)}, f32[7,256,256]{2,1,0:T(8,128)}, f32[8,128]{1,0:T(8,128)}, ...) custom-call(s32[4,2]{1,0:T(4,128)} %broadcast_subtract_fusion.place,, ...), custom_call_target="tpu_custom_call" | custom-call | tf_op jit(solution)/shard_map/pallas_call | solution.py:256
  37.4 0.0 copy-done.2
  37.4 0.0 copy-start.1
  37.4 1.6 %copy-done.1 = f32[4,2,2,2,128,128]{5,4,3,2,1,0:T(8,128)S(1)} copy-done((f32[4,2,2,2,128,128]{5,4,3,2,1,0:T(8,128)S(1)}, f32[4,2,2,2,128,128]{5,4,3,2,1,0:T(8,128)}, u32[]{:S(2)}) %copy-start.1) | copy-done | bytes 2097176
  39.0 1.2 shard_map.112.canvas_in
  40.2 0.0 copy-start
  40.2 2.7 %copy-done = f32[2,7,896,128]{3,2,1,0:T(8,128)} copy-done((f32[2,7,896,128]{3,2,1,0:T(8,128)}, f32[2,7,896,128]{3,2,1,0:T(8,128)S(1)}, u32[]{:S(2)}) %copy-start) | copy-done | bytes 6422552
  42.9 65.5 %shard_map.113 = (f32[2,7,896,128]{3,2,1,0:T(8,128)}, f32[6,256,256]{2,1,0:T(8,128)}) custom-call(f32[2,7,896,128]{3,2,1,0:T(8,128)} %copy-done, f32[7,256,256]{2,1,0:T(8,128)} %get-tuple-element.18.sums, f32[6,256,256]{2,1,0:T(8,128)} %bitcast.4, f32[8,128]{1,0:T(8,128)} %get-tuple-element.19.count, f32[2,768,768]{2,1,0:T(8,128)} %obj.3, ...), custom_call_target="tpu_custom_call" | custom-call | tf_op jit(solution)/shard_map/pallas_call | solution.py:681
  108.4 6.4 %shard_map.114 = (f32[2,768,768]{2,1,0:T(8,128)}, f32[4,2,256,256]{3,2,1,0:T(8,128)}) custom-call(s32[4,2]{1,0:T(4,128)} %broadcast_subtract_fusion.place, f32[2,7,896,128]{3,2,1,0:T(8,128)} %get-tuple-element.24.field), custom_call_target="tpu_custom_call" | custom-call | tf_op jit(solution)/shard_map/pallas_call | solution.py:750
  114.9 0.0 copy-start.3
  114.9 6.2 %copy.15 = f32[4,3,2,256,256]{4,3,2,1,0:T(8,128)} copy(f32[4,3,2,256,256]{4,3,2,1,0:T(8,128)} %get-tuple-element.32) | data formatting | bytes 12582912
  121.1 0.0 copy-done.3
  121.1 1.1 copy.16
Async XLA Ops:
  2.1 35.3 %copy-start.2 = (s32[4,2]{1,0:T(4,128)S(1)}, s32[4,2]{1,0:T(4,128)}, u32[]{:S(2)}) copy-start(s32[4,2]{1,0:T(4,128)} %broadcast_subtract_fusion.place) | copy-start | bytes 100
  37.4 1.6 %copy-start.1 = (f32[4,2,2,2,128,128]{5,4,3,2,1,0:T(8,128)S(1)}, f32[4,2,2,2,128,128]{5,4,3,2,1,0:T(8,128)}, u32[]{:S(2)}) copy-start(f32[4,2,2,2,128,128]{5,4,3,2,1,0:T(8,128)} %get-tuple-element.17.parts_in) | copy-start | bytes 6291460
  40.2 2.7 %copy-start = (f32[2,7,896,128]{3,2,1,0:T(8,128)}, f32[2,7,896,128]{3,2,1,0:T(8,128)S(1)}, u32[]{:S(2)}) copy-start(f32[2,7,896,128]{3,2,1,0:T(8,128)S(1)} %shard_map.112.canvas_in) | copy-start | bytes 19267588
  114.9 6.2 %copy-start.3 = (f32[6,256,256]{2,1,0:T(8,128)S(1)}, f32[6,256,256]{2,1,0:T(8,128)}, u32[]{:S(2)}) copy-start(f32[6,256,256]{2,1,0:T(8,128)} %get-tuple-element.26) | copy-start | bytes 4718596
